TPU v7x, 32 devices: a whole 2x2x4 slice. The times are simulated.
32 devices in a mesh: groups: 2 (over y), tm: 16 (over z, x, core).
Axes of the slice: x: 2, y: 2, z: 4, core: 2. Of those that a mesh axis runs over, the one named last changes fastest.
Arguments:
- features: bfloat16 [131072, 256], P(('groups', 'tm')), parts along dimension 0, may hold values from -6 to 6
- segment: int32 [131072], P(('groups', 'tm')), parts along dimension 0, may hold values from 0 to 63, never falling along the last dimension, each value on 1 to 8192 neighbouring positions
- w_first: bfloat16 [768, 256], replicated, may hold values from -0.21875 to 0.21875
- w_second: bfloat16 [768, 256], replicated, may hold values from -0.21875 to 0.21875
- w_head: bfloat16 [256, 32], replicated, may hold values from -0.375 to 0.375
- targets: float32 [131072, 32], P(('groups', 'tm')), parts along dimension 0, may hold values from -6 to 6
Outputs:
- hidden: bfloat16 [131072, 256], P(('groups', 'tm')), parts along dimension 0
- grad_features: bfloat16 [131072, 256], P(('groups', 'tm')), parts along dimension 0
- grad_first: float32 [1536, 256], P('groups'), parts along dimension 0
- grad_second: float32 [1536, 256], P('groups'), parts along dimension 0
- grad_head: float32 [512, 32], P('groups'), parts along dimension 0
- loss: float32 [2], P('groups'), parts along dimension 0
There are 2 independent parts, one for each index of `groups`. A program takes and returns all parts, laid end to end along the dimension named above; an argument that names none is the same for every part. Nothing has to cross between parts.
Inputs may be any that keep to these rules, and one draw needn't show every extreme that they name: Segment numbers never fall along time; each segment covers 1 to 8192 samples, one exactly 8192.
All inputs are finite; a program needn't handle non-finite values.
Results may differ from a plain program's by a relative error of at most 0.0075.
Values may be sent and summed in bfloat16 or wider, within the bound.
A program may use at most 128 MiB of HBM per device.

v0:
```python
import jax
import jax.numpy as jnp
from jax import lax
from jax.sharding import PartitionSpec as P

D_FIRST = 4
D_SECOND = 16


def padded_2(cells, sides, width):
    for axis, dim in sides:
        count = lax.axis_size(axis)
        ends = count - 1
        head = lax.slice_in_dim(cells, 0, width, axis=dim)
        tail = lax.slice_in_dim(cells, cells.shape[dim] - width, cells.shape[dim], axis=dim)
        cells = jnp.concatenate(
            [
                lax.ppermute(tail, axis, [(i, (i + 1) % count) for i in range(ends)]),
                cells,
                lax.ppermute(head, axis, [((i + 1) % count, i) for i in range(ends)]),
            ],
            axis=dim,
        )
    return cells


def tap_stack(padded, seg_pad, margin, dilation, rows):
    center = seg_pad[margin : margin + rows]
    pieces = []
    for tap in range(3):
        start = margin + (tap - 1) * dilation
        keep = (seg_pad[start : start + rows] == center)[:, None]
        pieces.append(jnp.where(keep, padded[start : start + rows], jnp.zeros((), padded.dtype)))
    return jnp.concatenate(pieces, 1)


def back_stack(padded, seg_pad, margin, dilation, rows):
    center = seg_pad[margin : margin + rows]
    pieces = []
    for tap in range(3):
        start = margin - (tap - 1) * dilation
        keep = (seg_pad[start : start + rows] == center)[:, None]
        pieces.append(jnp.where(keep, padded[start : start + rows], jnp.zeros((), padded.dtype)))
    return jnp.concatenate(pieces, 1)


def flipped(weight):
    width = weight.shape[1]
    return jnp.swapaxes(weight.reshape(3, width, width), 1, 2).reshape(3 * width, width)


def shards(features, segment, w_first, w_second, w_head, targets):
    local_rows = features.shape[0]
    total_rows = local_rows * lax.axis_size("tm")
    margin = D_FIRST + D_SECOND
    seg_pad = padded_2(segment + 1, (("tm", 0),), margin)
    seg_first = seg_pad[D_SECOND : D_SECOND + local_rows + 2 * D_FIRST]
    seg_second = seg_pad[D_FIRST : D_FIRST + local_rows + 2 * D_SECOND]
    feat_pad = padded_2(features, (("tm", 0),), D_FIRST)
    first_in = tap_stack(feat_pad, seg_first, D_FIRST, D_FIRST, local_rows)
    pre_first = jnp.dot(first_in, w_first, preferred_element_type=jnp.float32)
    act_first = jnp.maximum(pre_first, 0.0).astype(jnp.bfloat16)
    act_pad = padded_2(act_first, (("tm", 0),), D_SECOND)
    second_in = tap_stack(act_pad, seg_second, D_SECOND, D_SECOND, local_rows)
    pre_second = jnp.dot(second_in, w_second, preferred_element_type=jnp.float32)
    hidden = (features.astype(jnp.float32) + pre_second).astype(jnp.bfloat16)
    error = jnp.dot(hidden, w_head, preferred_element_type=jnp.float32) - targets
    error_sum = jnp.sum(error * error)
    scale = 1.0 / total_rows**0.5
    grad_out = (error * scale).astype(jnp.bfloat16)
    grad_head = jnp.dot(hidden.T, grad_out, preferred_element_type=jnp.float32)
    grad_hidden = jnp.dot(grad_out, w_head.T, preferred_element_type=jnp.float32)
    grad_pre2 = grad_hidden.astype(jnp.bfloat16)
    grad_second = jnp.dot(second_in.T, grad_pre2, preferred_element_type=jnp.float32)
    grad_pad2 = padded_2(grad_pre2, (("tm", 0),), D_SECOND)
    grad_act = jnp.dot(
        back_stack(grad_pad2, seg_second, D_SECOND, D_SECOND, local_rows),
        flipped(w_second),
        preferred_element_type=jnp.float32,
    )
    grad_pre1 = jnp.where(pre_first > 0, grad_act, 0.0).astype(jnp.bfloat16)
    grad_pad1 = padded_2(grad_pre1, (("tm", 0),), D_FIRST)
    grad_first = jnp.dot(first_in.T, grad_pre1, preferred_element_type=jnp.float32)
    grad_features = grad_hidden + jnp.dot(
        back_stack(grad_pad1, seg_first, D_FIRST, D_FIRST, local_rows),
        flipped(w_first),
        preferred_element_type=jnp.float32,
    )
    grad_first, grad_second, grad_head, error_sum = lax.psum(
        (grad_first, grad_second, grad_head, error_sum), "tm"
    )
    loss = jnp.reshape(error_sum / (total_rows * w_head.shape[1]), (1,))
    return (hidden, grad_features.astype(jnp.bfloat16), grad_first, grad_second, grad_head, loss)


def solution(mesh):
    return jax.shard_map(
        shards,
        mesh=mesh,
        in_specs=(
            P(("groups", "tm"), None),
            P(("groups", "tm")),
            P(),
            P(),
            P(),
            P(("groups", "tm"), None),
        ),
        out_specs=(
            P(("groups", "tm"), None),
            P(("groups", "tm"), None),
            P("groups", None),
            P("groups", None),
            P("groups", None),
            P("groups"),
        ),
        check_vma=False,
    )
```

profile of v0, /device:TPU:0, one launch (start us, length us, event | category | flops | bytes accessed | tf_op | source)
XLA Modules:
  0.0 245.3 jit_solution(15057422130377659170)
XLA Ops:
  7.2 0.0 copy-start
  7.2 0.0 all-reduce.4.cloned.1.call-start
  7.2 0.7 broadcast_add_fusion
  7.9 0.1 fusion.56
  8.0 2.3 collective-permute-start
  10.4 1.3 collective-permute-start.2
  11.7 0.7 fusion.55
  12.4 5.1 %collective-permute-start.1 = (bf16[4,256]{1,0:T(4,128)(2,1)S(1)}, bf16[4,256]{1,0:T(4,128)(2,1)S(1)}, u32[]{:S(2)}, u32[]{:S(2)}) collective-permute-start(bf16[4,256]{1,0:T(4,128)(2,1)S(1)} %get-tuple-element.24), channel_id=1, source_target_pairs={{0,1},{1,2},{2,3},{3,4},{4,5},{5,6},{6,7},{7,8},{8,9},{9,10},{10,1... | collective-permute-start | bytes 6152 | tf_op jit(solution)/shard_map/ppermute | solution.py:18
  17.5 1.3 collective-permute-start.3
  18.8 0.0 collective-permute-done
  18.8 0.1 fusion.41
  19.0 2.9 %collective-permute-done.3 = bf16[4,256]{1,0:T(4,128)(2,1)S(1)} collective-permute-done((bf16[4,256]{1,0:T(4,128)(2,1)S(1)}, bf16[4,256]{1,0:T(4,128)(2,1)S(1)}, u32[]{:S(2)}, u32[]{:S(2)}) %collective-permute-start.3) | collective-permute-done | bytes 2080 | tf_op jit(solution)/shard_map/ppermute | solution.py:20
  21.8 6.6 %fusion.35 = (bf16[4096,256]{1,0:T(8,128)(2,1)S(1)}, bf16[4096,256]{1,0:T(8,128)(2,1)S(1)}) fusion(bf16[4096,256]{1,0:T(8,128)(2,1)} %param.6, bf16[4,256]{1,0:T(4,128)(2,1)S(1)} %collective-permute-done.1, pred[4096]{0:T(1024)(128)(4,1)S(1)} %get-tuple-element.27, bf16[4,256]{1,0:T(4,128)(2,1)S(1)} %collective-permute-done.3, ...), kind=kLoop, calls=%fused_computation.40 | loop fusion | flops 10485760 | bytes 6303744 | tf_op jit(solution)/shard_map/jit(_where)/select_n | solution.py:33
  28.5 0.0 copy-start.17
  28.5 4.4 %maximum_convert_fusion = (bf16[4096,256]{1,0:T(8,128)(2,1)S(1)}, f32[4096,256]{1,0:T(8,128)}) fusion(bf16[768,256]{1,0:T(8,128)(2,1)S(1)} %copy-done.16, bf16[4096,256]{1,0:T(8,128)(2,1)S(1)} %get-tuple-element.23, bf16[4096,256]{1,0:T(8,128)(2,1)S(1)} %copy-done.5, bf16[4096,256]{1,0:T(8,128)(2,1)S(1)} %get-tuple-element.22), kind=kOutput, calls=%fused_computation.21 | convolution fusion | flops 1631584256 | bytes 12976128 | tf_op jit(solution)/shard_map/dot_general | solution.py:61
  32.9 4.3 %collective-permute-start.4 = (bf16[16,256]{1,0:T(8,128)(2,1)S(1)}, bf16[16,256]{1,0:T(8,128)(2,1)S(1)}, u32[]{:S(2)}, u32[]{:S(2)}) collective-permute-start(bf16[16,256]{1,0:T(8,128)(2,1)S(1)} %get-tuple-element.20), channel_id=1, source_target_pairs={{0,1},{1,2},{2,3},{3,4},{4,5},{5,6},{6,7},{7,8},{8,9},{9,10},{10,1... | collective-permute-start | bytes 24584 | tf_op jit(solution)/shard_map/ppermute | solution.py:18
  37.2 1.3 collective-permute-start.5
  38.5 0.9 copy.12
  39.4 0.2 copy.13
  39.6 0.7 collective-permute-done.5
  40.2 6.4 %fusion.33 = (bf16[4096,256]{1,0:T(8,128)(2,1)S(1)}, bf16[4096,256]{1,0:T(8,128)(2,1)S(1)}) fusion(bf16[4096,256]{1,0:T(8,128)(2,1)S(1)} %get-tuple-element.34, bf16[16,256]{1,0:T(8,128)(2,1)S(1)} %collective-permute-done.4, pred[4096]{0:T(1024)(128)(4,1)S(1)} %get-tuple-element.26, bf16[16,256]{1,0:T(8,128)(2,1)S(1)} %collective-permute-done.5, ...), kind=kLoop, calls=%fused_computation.36 | loop fusion | flops 10485760 | bytes 6316032 | tf_op jit(solution)/shard_map/jit(_where)/select_n | solution.py:33
  46.7 0.0 copy-start.15
  46.7 2.3 fusion.18
  49.0 0.0 copy-start.1
  49.0 1.3 multiply_reduce_fusion
  50.4 0.4 fusion.36
  50.8 0.0 copy-done.1
  50.8 0.0 copy-start.4
  50.8 2.7 %fusion.57 = (bf16[4096,256]{1,0:T(8,128)(2,1)S(1)}, f32[4096,256]{1,0:T(8,128)}) fusion(bf16[256,32]{0,1:T(8,128)(2,1)S(1)} %copy-done, f32[4096,32]{0,1:T(8,128)S(1)} %get-tuple-element.39), kind=kOutput, calls=%fused_computation.71 | convolution fusion | flops 68419584 | bytes 6832128 | tf_op jit(solution)/shard_map/dot_general | solution.py:72
  53.6 2.7 %fusion.25 = f32[768,256]{1,0:T(8,128)} fusion(bf16[4096,256]{1,0:T(8,128)(2,1)S(1)} %get-tuple-element.36, bf16[4096,256]{1,0:T(8,128)(2,1)S(1)} %get-tuple-element.19, bf16[4096,256]{1,0:T(8,128)(2,1)S(1)} %copy-done.4, bf16[4096,256]{1,0:T(8,128)(2,1)S(1)} %get-tuple-element.18), kind=kOutput, calls=%fused_computation.22 | convolution fusion | flops 1629487104 | bytes 9175040 | tf_op jit(solution)/shard_map/dot_general | solution.py:74
  56.3 1.3 collective-permute-start.6
  57.6 6.2 %collective-permute-start.7 = (bf16[16,256]{1,0:T(8,128)(2,1)S(1)}, bf16[16,256]{1,0:T(8,128)(2,1)S(1)}, u32[]{:S(2)}, u32[]{:S(2)}) collective-permute-start(bf16[16,256]{1,0:T(8,128)(2,1)S(1)} %get-tuple-element.17), channel_id=1, source_target_pairs={{0,1},{1,2},{2,3},{3,4},{4,5},{5,6},{6,7},{7,8},{8,9},{9,10},{10,1... | collective-permute-start | bytes 24584 | tf_op jit(solution)/shard_map/ppermute | solution.py:18
  63.8 60.5 %all-reduce = (f32[256,32]{0,1:T(8,128)}, f32[]{:T(128)}) all-reduce(f32[256,32]{0,1:T(8,128)S(1)} %fusion.36, f32[]{:T(128)} %get-tuple-element.38), channel_id=1, replica_groups=mesh['groups'=2,'tm'=16] {'tm'}, use_global_device_ids=true, to_apply=%region_2.3 | all-reduce | flops 8193 | bytes 65544 | tf_op jit(solution)/shard_map/psum | solution.py:89
  124.9 0.0 copy-start.18
  125.0 6.4 %fusion.31 = (bf16[4096,256]{1,0:T(8,128)(2,1)S(1)}, bf16[4096,256]{1,0:T(8,128)(2,1)S(1)}) fusion(bf16[16,256]{1,0:T(8,128)(2,1)S(1)} %collective-permute-done.6, bf16[4096,256]{1,0:T(8,128)(2,1)S(1)} %get-tuple-element.36, pred[4096]{0:T(1024)(128)(4,1)S(1)} %get-tuple-element.31, bf16[16,256]{1,0:T(8,128)(2,1)S(1)} %collective-permute-done.7, ...), kind=kLoop, calls=%fused_computation.32 | loop fusion | flops 10485760 | bytes 6316032 | tf_op jit(solution)/shard_map/jit(_where)/select_n | solution.py:43
  131.4 0.0 copy-start.7
  131.5 2.3 fusion.22
  133.8 0.0 copy-start.8
  133.8 1.3 collective-permute-start.8
  135.1 3.2 %collective-permute-start.9 = (bf16[4,256]{1,0:T(4,128)(2,1)S(1)}, bf16[4,256]{1,0:T(4,128)(2,1)S(1)}, u32[]{:S(2)}, u32[]{:S(2)}) collective-permute-start(bf16[4,256]{1,0:T(4,128)(2,1)S(1)} %get-tuple-element.13), channel_id=1, source_target_pairs={{0,1},{1,2},{2,3},{3,4},{4,5},{5,6},{6,7},{7,8},{8,9},{9,10},{10,1... | collective-permute-start | bytes 6152 | tf_op jit(solution)/shard_map/ppermute | solution.py:18
  138.4 2.7 %fusion.26 = f32[768,256]{1,0:T(8,128)} fusion(bf16[4096,256]{1,0:T(8,128)(2,1)S(1)} %fusion.22, bf16[4096,256]{1,0:T(8,128)(2,1)S(1)} %copy-done.13, bf16[4096,256]{1,0:T(8,128)(2,1)S(1)} %copy-done.7, bf16[4096,256]{1,0:T(8,128)(2,1)S(1)} %copy-done.11), kind=kOutput, calls=%fused_computation.23 | convolution fusion | flops 1629487104 | bytes 9175040 | tf_op jit(solution)/shard_map/dot_general | solution.py:83
  141.1 0.0 all-reduce.4.cloned.1.call-update
  141.1 0.0 copy-start.9
  141.2 7.2 %fusion.29 = (bf16[4096,256]{1,0:T(8,128)(2,1)S(1)}, bf16[4096,256]{1,0:T(8,128)(2,1)S(1)}) fusion(bf16[4,256]{1,0:T(4,128)(2,1)S(1)} %collective-permute-done.8, bf16[4096,256]{1,0:T(8,128)(2,1)} %copy-done.8, pred[4096]{0:T(1024)(128)(4,1)S(1)} %get-tuple-element.30, bf16[4,256]{1,0:T(4,128)(2,1)S(1)} %collective-permute-done.9, ...), kind=kLoop, calls=%fused_computation.28 | loop fusion | flops 10485760 | bytes 6303744 | tf_op jit(solution)/shard_map/jit(_where)/select_n | solution.py:43
  148.4 3.1 %fusion.15 = bf16[4096,256]{1,0:T(8,128)(2,1)} fusion(f32[4096,256]{1,0:T(8,128)S(1)} %copy-done.2, bf16[768,256]{1,0:T(8,128)(2,1)S(1)} %bitcast.21, bf16[4096,256]{1,0:T(8,128)(2,1)S(1)} %get-tuple-element.11, bf16[4096,256]{1,0:T(8,128)(2,1)S(1)} %copy-done.9, bf16[4096,256]{1,0:T(8,128)(2,1)S(1)} %get-tuple-element.10), kind=kOutput, calls=%fused_computation.16 | convolution fusion | flops 1631584256 | bytes 12976128 | tf_op jit(solution)/shard_map/dot_general | solution.py:84
  151.4 82.8 %all-reduce.4.cloned.1.call-done = (f32[768,256]{1,0:T(8,128)}, f32[768,256]{1,0:T(8,128)}) async-done(((f32[768,256]{1,0:T(8,128)}, f32[768,256]{1,0:T(8,128)}), (f32[768,256]{1,0:T(8,128)}, f32[768,256]{1,0:T(8,128)})) %all-reduce.4.cloned.1.call-update) | async-done | bytes 1572880 | tf_op jit(solution)/shard_map/psum | solution.py:89
  234.3 2.1 copy.16
  236.4 0.9 copy.17
  (40 shorter events, 0.1 us)
Async XLA Ops:
  7.2 41.8 %copy-start = (bf16[256,32]{0,1:T(8,128)(2,1)S(1)}, bf16[256,32]{0,1:T(8,128)(2,1)}, u32[]{:S(2)}) copy-start(bf16[256,32]{0,1:T(8,128)(2,1)} %param.10) | copy-start | bytes 49156
  7.2 227.1 %all-reduce.4.cloned.1.call-start = ((), (), s32[]{:S(2)}) async-start(), calls=%async_computation | async-start | bytes 3145728 | tf_op jit(solution)/shard_map/psum | solution.py:89
  8.0 10.8 %collective-permute-start = (s32[20]{0:T(128)S(1)}, s32[20]{0:T(128)S(1)}, u32[]{:S(2)}, u32[]{:S(2)}) collective-permute-start(s32[20]{0:T(128)S(1)} %get-tuple-element.32), channel_id=1, source_target_pairs={{0,1},{1,2},{2,3},{3,4},{4,5},{5,6},{6,7},{7,8},{8,9},{9,10},{10,1... | collective-permute-start | bytes 248 | tf_op jit(solution)/shard_map/ppermute | solution.py:18
  10.4 8.5 %collective-permute-start.2 = (s32[20]{0:T(128)S(1)}, s32[20]{0:T(128)S(1)}, u32[]{:S(2)}, u32[]{:S(2)}) collective-permute-start(s32[20]{0:T(128)S(1)} %get-tuple-element.33), channel_id=1, source_target_pairs={{1,0},{2,1},{3,2},{4,3},{5,4},{6,5},{7,6},{8,7},{9,8},{10,9},{11,1... | collective-permute-start | bytes 248 | tf_op jit(solution)/shard_map/ppermute | solution.py:20
  12.4 6.6 %collective-permute-start.1 = (bf16[4,256]{1,0:T(4,128)(2,1)S(1)}, bf16[4,256]{1,0:T(4,128)(2,1)S(1)}, u32[]{:S(2)}, u32[]{:S(2)}) collective-permute-start(bf16[4,256]{1,0:T(4,128)(2,1)S(1)} %get-tuple-element.24), channel_id=1, source_target_pairs={{0,1},{1,2},{2,3},{3,4},{4,5},{5,6},{6,7},{7,8},{8,9},{9,10},{10,1... | collective-permute-start | bytes 6152 | tf_op jit(solution)/shard_map/ppermute | solution.py:18
  17.5 4.3 %collective-permute-start.3 = (bf16[4,256]{1,0:T(4,128)(2,1)S(1)}, bf16[4,256]{1,0:T(4,128)(2,1)S(1)}, u32[]{:S(2)}, u32[]{:S(2)}) collective-permute-start(bf16[4,256]{1,0:T(4,128)(2,1)S(1)} %get-tuple-element.25), channel_id=1, source_target_pairs={{1,0},{2,1},{3,2},{4,3},{5,4},{6,5},{7,6},{8,7},{9,8},{10,9},{11,1... | collective-permute-start | bytes 6152 | tf_op jit(solution)/shard_map/ppermute | solution.py:20
  21.8 6.7 %copy-start.5 = (bf16[4096,256]{1,0:T(8,128)(2,1)S(1)}, bf16[4096,256]{1,0:T(8,128)(2,1)}, u32[]{:S(2)}) copy-start(bf16[4096,256]{1,0:T(8,128)(2,1)} %param.6) | copy-start | bytes 6291460
  21.8 6.7 %copy-start.16 = (bf16[768,256]{1,0:T(8,128)(2,1)S(1)}, bf16[768,256]{1,0:T(8,128)(2,1)}, u32[]{:S(2)}) copy-start(bf16[768,256]{1,0:T(8,128)(2,1)} %param.8) | copy-start | bytes 1179652
  28.4 4.4 %copy-start.10 = (bf16[4096,256]{1,0:T(8,128)(2,1)}, bf16[4096,256]{1,0:T(8,128)(2,1)S(1)}, u32[]{:S(2)}) copy-start(bf16[4096,256]{1,0:T(8,128)(2,1)S(1)} %get-tuple-element.22) | copy-start | bytes 6291460
  28.5 4.4 %copy-start.12 = (bf16[4096,256]{1,0:T(8,128)(2,1)}, bf16[4096,256]{1,0:T(8,128)(2,1)S(1)}, u32[]{:S(2)}) copy-start(bf16[4096,256]{1,0:T(8,128)(2,1)S(1)} %get-tuple-element.23) | copy-start | bytes 6291460
  28.5 10.0 %copy-start.17 = (bf16[768,256]{1,0:T(8,128)(2,1)S(1)}, bf16[768,256]{1,0:T(8,128)(2,1)}, u32[]{:S(2)}) copy-start(bf16[768,256]{1,0:T(8,128)(2,1)} %param.9) | copy-start | bytes 1179652
  32.9 13.8 %copy-start.3 = (bf16[4096,256]{1,0:T(8,128)(2,1)}, bf16[4096,256]{1,0:T(8,128)(2,1)S(1)}, u32[]{:S(2)}) copy-start(bf16[4096,256]{1,0:T(8,128)(2,1)S(1)} %get-tuple-element.34) | copy-start | bytes 6291460
  32.9 6.7 %collective-permute-start.4 = (bf16[16,256]{1,0:T(8,128)(2,1)S(1)}, bf16[16,256]{1,0:T(8,128)(2,1)S(1)}, u32[]{:S(2)}, u32[]{:S(2)}) collective-permute-start(bf16[16,256]{1,0:T(8,128)(2,1)S(1)} %get-tuple-element.20), channel_id=1, source_target_pairs={{0,1},{1,2},{2,3},{3,4},{4,5},{5,6},{6,7},{7,8},{8,9},{9,10},{10,1... | collective-permute-start | bytes 24584 | tf_op jit(solution)/shard_map/ppermute | solution.py:18
  37.2 3.1 %collective-permute-start.5 = (bf16[16,256]{1,0:T(8,128)(2,1)S(1)}, bf16[16,256]{1,0:T(8,128)(2,1)S(1)}, u32[]{:S(2)}, u32[]{:S(2)}) collective-permute-start(bf16[16,256]{1,0:T(8,128)(2,1)S(1)} %get-tuple-element.21), channel_id=1, source_target_pairs={{1,0},{2,1},{3,2},{4,3},{5,4},{6,5},{7,6},{8,7},{9,8},{10,9},{11,1... | collective-permute-start | bytes 24584 | tf_op jit(solution)/shard_map/ppermute | solution.py:20
  40.2 6.4 %copy-start.6 = (bf16[4096,256]{1,0:T(8,128)(2,1)S(1)}, bf16[4096,256]{1,0:T(8,128)(2,1)}, u32[]{:S(2)}) copy-start(bf16[4096,256]{1,0:T(8,128)(2,1)} %param.6) | copy-start | bytes 6291460
  46.7 2.4 copy-start.15
  49.0 1.8 copy-start.1
  50.8 2.7 %copy-start.4 = (bf16[4096,256]{1,0:T(8,128)(2,1)S(1)}, bf16[4096,256]{1,0:T(8,128)(2,1)}, u32[]{:S(2)}) copy-start(bf16[4096,256]{1,0:T(8,128)(2,1)} %copy-done.3) | copy-start | bytes 6291460
  56.3 68.6 %collective-permute-start.6 = (bf16[16,256]{1,0:T(8,128)(2,1)S(1)}, bf16[16,256]{1,0:T(8,128)(2,1)S(1)}, u32[]{:S(2)}, u32[]{:S(2)}) collective-permute-start(bf16[16,256]{1,0:T(8,128)(2,1)S(1)} %get-tuple-element.16), channel_id=1, source_target_pairs={{1,0},{2,1},{3,2},{4,3},{5,4},{6,5},{7,6},{8,7},{9,8},{10,9},{11,1... | collective-permute-start | bytes 24584 | tf_op jit(solution)/shard_map/ppermute | solution.py:20
  57.6 67.4 %collective-permute-start.7 = (bf16[16,256]{1,0:T(8,128)(2,1)S(1)}, bf16[16,256]{1,0:T(8,128)(2,1)S(1)}, u32[]{:S(2)}, u32[]{:S(2)}) collective-permute-start(bf16[16,256]{1,0:T(8,128)(2,1)S(1)} %get-tuple-element.17), channel_id=1, source_target_pairs={{0,1},{1,2},{2,3},{3,4},{4,5},{5,6},{6,7},{7,8},{8,9},{9,10},{10,1... | collective-permute-start | bytes 24584 | tf_op jit(solution)/shard_map/ppermute | solution.py:18
  124.9 6.5 %copy-start.18 = (bf16[3,256,256]{2,1,0:T(8,128)(2,1)S(1)}, bf16[3,256,256]{2,1,0:T(8,128)(2,1)}, u32[]{:S(2)}) copy-start(bf16[3,256,256]{2,1,0:T(8,128)(2,1)} %copy.12) | copy-start | bytes 1179652
  124.9 6.5 %copy-start.19 = (f32[4096,256]{1,0:T(8,128)S(1)}, f32[4096,256]{1,0:T(8,128)}, u32[]{:S(2)}) copy-start(f32[4096,256]{1,0:T(8,128)} %get-tuple-element.35) | copy-start | bytes 12582916
  131.4 6.9 %copy-start.7 = (bf16[4096,256]{1,0:T(8,128)(2,1)S(1)}, bf16[4096,256]{1,0:T(8,128)(2,1)}, u32[]{:S(2)}) copy-start(bf16[4096,256]{1,0:T(8,128)(2,1)} %param.6) | copy-start | bytes 6291460
  131.4 6.9 %copy-start.11 = (bf16[4096,256]{1,0:T(8,128)(2,1)S(1)}, bf16[4096,256]{1,0:T(8,128)(2,1)}, u32[]{:S(2)}) copy-start(bf16[4096,256]{1,0:T(8,128)(2,1)} %copy-done.10) | copy-start | bytes 6291460
  131.4 6.9 %copy-start.13 = (bf16[4096,256]{1,0:T(8,128)(2,1)S(1)}, bf16[4096,256]{1,0:T(8,128)(2,1)}, u32[]{:S(2)}) copy-start(bf16[4096,256]{1,0:T(8,128)(2,1)} %copy-done.12) | copy-start | bytes 6291460
  133.8 4.5 %copy-start.8 = (bf16[4096,256]{1,0:T(8,128)(2,1)}, bf16[4096,256]{1,0:T(8,128)(2,1)S(1)}, u32[]{:S(2)}) copy-start(bf16[4096,256]{1,0:T(8,128)(2,1)S(1)} %fusion.22) | copy-start | bytes 6291460
  133.8 7.3 %collective-permute-start.8 = (bf16[4,256]{1,0:T(4,128)(2,1)S(1)}, bf16[4,256]{1,0:T(4,128)(2,1)S(1)}, u32[]{:S(2)}, u32[]{:S(2)}) collective-permute-start(bf16[4,256]{1,0:T(4,128)(2,1)S(1)} %get-tuple-element.12), channel_id=1, source_target_pairs={{1,0},{2,1},{3,2},{4,3},{5,4},{6,5},{7,6},{8,7},{9,8},{10,9},{11,1... | collective-permute-start | bytes 6152 | tf_op jit(solution)/shard_map/ppermute | solution.py:20
  135.1 6.0 %collective-permute-start.9 = (bf16[4,256]{1,0:T(4,128)(2,1)S(1)}, bf16[4,256]{1,0:T(4,128)(2,1)S(1)}, u32[]{:S(2)}, u32[]{:S(2)}) collective-permute-start(bf16[4,256]{1,0:T(4,128)(2,1)S(1)} %get-tuple-element.13), channel_id=1, source_target_pairs={{0,1},{1,2},{2,3},{3,4},{4,5},{5,6},{6,7},{7,8},{8,9},{9,10},{10,1... | collective-permute-start | bytes 6152 | tf_op jit(solution)/shard_map/ppermute | solution.py:18
  141.1 7.2 %copy-start.2 = (f32[4096,256]{1,0:T(8,128)S(1)}, f32[4096,256]{1,0:T(8,128)}, u32[]{:S(2)}) copy-start(f32[4096,256]{1,0:T(8,128)} %get-tuple-element.37) | copy-start | bytes 12582916
  141.1 7.2 %copy-start.9 = (bf16[4096,256]{1,0:T(8,128)(2,1)S(1)}, bf16[4096,256]{1,0:T(8,128)(2,1)}, u32[]{:S(2)}) copy-start(bf16[4096,256]{1,0:T(8,128)(2,1)} %copy-done.8) | copy-start | bytes 6291460
  234.3 2.1 copy-start.14
Sparse Core Ops, SparseCore 0:
  141.2 92.9 all-reduce.3
where the time goes:
time: 246 us; the launch traced here: 245 us
  waiting for transfers between devices  86.4 us (35%)
  blocking collectives  60.5 us (25%)
  starting transfers between devices  27.6 us (11%)
  other arithmetic  27.4 us (11%)
  matrix products  22.1 us (9%)
  between operations  16.3 us (7%)
  local copies, waits for them, and re-layouts  5.01 us (2%)
    psum x1, waiting for transfers between devices, shards(): lax.psum((grad_first, grad_second, grad_head, error_sum), 'tm')  82.8 us
    psum x1, blocking collectives, shards(): lax.psum((grad_first, grad_second, grad_head, error_sum), 'tm')  60.5 us
    ppermute x5, starting transfers between devices, padded_2(): lax.ppermute(tail, axis, [(i, (i + 1) % count) for i in range(ends)])  21.1 us
    select_n x2, other arithmetic, back_stack(): jnp.where(keep, padded[start:start + rows], jnp.zeros((), padded.dtype))  13.6 us
    select_n x2, other arithmetic, tap_stack(): jnp.where(keep, padded[start:start + rows], jnp.zeros((), padded.dtype))  13 us
    ppermute x5, starting transfers between devices, padded_2(): lax.ppermute(head, axis, [((i + 1) % count, i) for i in range(ends)])  6.45 us
  transfers between devices with their start and end apart: 11, of which 3 were waited for; matrix products, arithmetic and copies ran while one was open for 6% of the time, Pallas kernels for 0%

commit v1 on v0

v1 whole, which is shorter than its diff:
```python
import functools

import jax
import jax.numpy as jnp
from jax import lax
from jax.experimental import pallas as pl
from jax.experimental.pallas import tpu as pltpu
from jax.sharding import PartitionSpec as P

D_FIRST = 4
D_SECOND = 16
EDGE = 128
GAP = 16
BASE = EDGE + GAP
HALO = 64
BF, F32 = jnp.bfloat16, jnp.float32
MESH = pl.DeviceIdType.MESH


def dot(a, b, ca=1, cb=0):
    return lax.dot_general(a, b, (((ca,), (cb,)), ((), ())), preferred_element_type=F32)


def compute(rows, scale, feat, flo, fhi, seg, tgt, tlo, thi, w1, w2, wht,
            hid, gfeat, g1, g2, gh, err,
            fb, f32, segc, msk, act, gp2, gp1, ghid, w1t, w2t, ght, sem):
    ch = w1.shape[1]
    total = rows + 2 * BASE
    step = min(512, rows)
    steps = rows // step

    copies = [
        pltpu.make_async_copy(feat, fb.at[pl.ds(BASE, rows)], sem.at[0]),
        pltpu.make_async_copy(flo, fb.at[pl.ds(BASE - HALO, HALO)], sem.at[1]),
        pltpu.make_async_copy(fhi, fb.at[pl.ds(BASE + rows, HALO)], sem.at[2]),
    ]
    for copy in copies:
        copy.start()

    diagonal = lax.broadcasted_iota(jnp.int32, (128, 128), 0) == lax.broadcasted_iota(
        jnp.int32, (128, 128), 1)
    ones = jnp.ones((256, 128), BF)

    def column(i, _):
        row = jnp.broadcast_to(seg[pl.ds(i, 1), :], (128, 128))
        low = row & 255
        high = row - low
        both = jnp.concatenate([jnp.where(diagonal, low, 0), jnp.where(diagonal, high, 0)], 1)
        segc[pl.ds(pl.multiple_of(GAP + i * 128, 16), 128), :] = dot(both.astype(F32).astype(BF), ones)
        return 0

    lax.fori_loop(0, seg.shape[0], column, 0)
    segc[0:GAP, :] = jnp.full((GAP, 128), -1.0, F32)
    segc[total - GAP:total, :] = jnp.full((GAP, 128), -1.0, F32)

    def masks(i, _):
        q = pl.multiple_of(GAP + i * 128, 16)
        around = segc.at[pl.ds(q - GAP, 128 + 2 * GAP), :]
        center = around[GAP:GAP + 128, :]
        for n, off in enumerate((-D_FIRST, D_FIRST, -D_SECOND, D_SECOND)):
            same = around[GAP + off:GAP + off + 128, :] == center
            msk[n, pl.ds(q, 128), :] = jnp.where(same, 1.0, 0.0).astype(BF)
        return 0

    lax.fori_loop(0, seg.shape[0], masks, 0)

    for k in range(3):
        w1t[k * ch:(k + 1) * ch, :] = w1[k * ch:(k + 1) * ch, :].T
        w2t[k * ch:(k + 1) * ch, :] = w2[k * ch:(k + 1) * ch, :].T
    for scratch, edge, kind in ((act, GAP, BF), (gp2, GAP, BF), (fb, BASE - HALO, BF), (gp1, EDGE, F32)):
        zero = jnp.zeros((edge, ch), kind)
        scratch[0:edge, :] = zero
        scratch[total - edge:total, :] = zero
    g1[...] = jnp.zeros_like(g1)
    g2[...] = jnp.zeros_like(g2)
    ght[...] = jnp.zeros_like(ght)
    err[...] = jnp.zeros_like(err)
    for copy in copies:
        copy.wait()

    def widen(q, size):
        f32[pl.ds(q, size), :] = fb[pl.ds(q, size), :].astype(F32)

    def mask(n, q, size):
        m = msk[n, pl.ds(q, size), :]
        return jnp.concatenate([m] * (ch // 128), 1)

    def near(wide, exact, q, size, back):
        around = wide.at[pl.ds(q - 8, size + 16), :]
        sides = (around[8 - D_FIRST:8 - D_FIRST + size, :].astype(BF) * mask(0, q, size),
                 around[8 + D_FIRST:8 + D_FIRST + size, :].astype(BF) * mask(1, q, size))
        low, high = sides[::-1] if back else sides
        return jnp.concatenate([low, exact, high], 1)

    def far(field, q, size, back):
        sides = (field[pl.ds(q - D_SECOND, size), :] * mask(2, q, size),
                 field[pl.ds(q + D_SECOND, size), :] * mask(3, q, size))
        low, high = sides[::-1] if back else sides
        return jnp.concatenate([low, field[pl.ds(q, size), :], high], 1)

    def first(q, size):
        x = near(f32, fb[pl.ds(q, size), :], q, size, False)
        act[pl.ds(q, size), :] = jnp.maximum(dot(x, w1[...]), 0.0).astype(BF)

    def second(q, size, targets):
        y = far(act, q, size, False)
        h = (f32[pl.ds(q, size), :] + dot(y, w2[...])).astype(BF)
        error = dot(wht[...], h, 1, 1) - targets
        gout = (error * scale).astype(BF)
        back = dot(gout, wht[...], 0, 0)
        gp2[pl.ds(q, size), :] = back.astype(BF)
        return h, error, gout, back

    def own(i):
        return (pl.multiple_of(i * step, step), pl.multiple_of(BASE + i * step, 16))

    def loop(body):
        lax.fori_loop(0, steps, lambda i, c: (body(*own(i)), c)[1], 0)

    last = BASE + rows
    widen(0, BASE)
    widen(last, BASE)
    loop(lambda t, q: widen(q, step))
    first(GAP, EDGE)
    first(last, EDGE)
    loop(lambda t, q: first(q, step))

    second(GAP, EDGE, tlo[...])
    second(last, EDGE, thi[...])

    def middle(t, q):
        h, error, gout, back = second(q, step, tgt[:, pl.ds(t, step)])
        hid[pl.ds(t, step), :] = h
        ghid[pl.ds(t, step), :] = back
        square = error * error
        part = square[:, 0:128]
        for j in range(1, step // 128):
            part = part + square[:, j * 128:(j + 1) * 128]
        err[...] += part
        ght[0:32, :] += dot(gout, h)

    loop(middle)

    def third(q, size):
        b = far(gp2, q, size, True)
        a = act[pl.ds(q, size), :]
        g = jnp.where(a > 0, dot(b, w2t[...]), 0.0)
        gp1[pl.ds(q, size), :] = g.astype(BF).astype(F32)
        return a, b

    third(EDGE, GAP)
    third(last, GAP)

    def outer(t, q):
        a, b = third(q, step)
        g2[...] += dot(a, b, 0, 0)

    loop(outer)

    def final(t, q):
        b = near(gp1, gp1[pl.ds(q, step), :].astype(BF), q, step, True)
        g1[...] += dot(fb[pl.ds(q, step), :], b, 0, 0)
        gfeat[pl.ds(t, step), :] = (ghid[pl.ds(t, step), :] + dot(b, w1t[...])).astype(BF)

    loop(final)
    gh[...] = ght[...].T


def local(features, flo, fhi, seg, tgt, tlo, thi, w_first, w_second, wht, scale):
    rows, ch = features.shape
    total = rows + 2 * BASE
    vmem = pl.BlockSpec(memory_space=pltpu.VMEM)
    anys = pl.BlockSpec(memory_space=pl.ANY)
    traits = wht.shape[0]
    flops = 2 * rows * ch * ch * 20
    return pl.pallas_call(
        functools.partial(compute, rows, scale),
        out_shape=[
            jax.ShapeDtypeStruct((rows, ch), BF),
            jax.ShapeDtypeStruct((rows, ch), BF),
            jax.ShapeDtypeStruct((ch, 3 * ch), F32),
            jax.ShapeDtypeStruct((ch, 3 * ch), F32),
            jax.ShapeDtypeStruct((ch, 128), F32),
            jax.ShapeDtypeStruct((traits, 128), F32),
        ],
        in_specs=[anys] * 3 + [vmem] * 7,
        out_specs=[vmem] * 6,
        scratch_shapes=[
            pltpu.VMEM((total, ch), BF),
            pltpu.VMEM((total, ch), F32),
            pltpu.VMEM((total, 128), F32),
            pltpu.VMEM((4, total, 128), BF),
            pltpu.VMEM((total, ch), BF),
            pltpu.VMEM((total, ch), BF),
            pltpu.VMEM((total, ch), F32),
            pltpu.VMEM((rows, ch), F32),
            pltpu.VMEM((3 * ch, ch), BF),
            pltpu.VMEM((3 * ch, ch), BF),
            pltpu.VMEM((128, ch), F32),
            pltpu.SemaphoreType.DMA((3,)),
        ],
        compiler_params=pltpu.CompilerParams(vmem_limit_bytes=56 * 2**20),
        cost_estimate=pl.CostEstimate(flops=flops, bytes_accessed=8 * rows * ch, transcendentals=0),
    )(features, flo, fhi, seg, tgt, tlo, thi, w_first, w_second, wht)


def total_kernel(g1, g2, gh, err, o1, o2, oh, oe,
                 out1, in1, part1, out2, in2, part2, in3, out3, res, eout, ein, ez, ssem, rsem):
    me = lax.axis_index("tm")
    group = lax.axis_index("groups")
    core, x, z = lax.rem(me, 2), lax.rem(me // 2, 2), me // 4

    def at(zz, xx, cc):
        return (group, (zz * 2 + xx) * 2 + cc)

    other_core = at(z, x, 1 - core)
    other_x = at(z, 1 - x, core)
    others_z = [at(lax.rem(z + k, 4), x, core) for k in (1, 2, 3)]

    barrier = pltpu.get_barrier_semaphore()
    for peer in [other_core, other_x] + others_z:
        pl.semaphore_signal(barrier, inc=1, device_id=peer, device_id_type=MESH)
    pl.semaphore_wait(barrier, 5)

    count = [0]

    def send(src, dst, peer):
        n = count[0]
        count[0] += 1
        copy = pltpu.make_async_remote_copy(
            src_ref=src, dst_ref=dst, send_sem=ssem.at[n], recv_sem=rsem.at[n],
            device_id=peer, device_id_type=MESH)
        copy.start()
        return copy

    sent = []
    wide = g2.shape[1]
    half, quarter, mine = 128, 64, 16
    c0 = pl.multiple_of(core * half, half)
    c1 = pl.multiple_of((1 - core) * half, half)
    x0 = pl.multiple_of(x * quarter, quarter)
    x1 = pl.multiple_of((1 - x) * quarter, quarter)
    z0 = pl.multiple_of(z * mine, mine)

    pieces = [(0, wide), (wide, wide + 128)]

    def load(piece, start):
        if piece == 0:
            return g2[pl.ds(start, half), :]
        return jnp.concatenate([g1[pl.ds(start, half), :], gh[pl.ds(start, half), :]], 1)

    def cols(ref, piece):
        start, size = pieces[piece]
        return ref.at[:, start:start + size]

    def step1(p):
        start, size = pieces[p]
        out1[:, start:start + size] = load(p, c1).astype(BF)
        return send(cols(out1, p), cols(in1, p), other_core)

    def step2(p):
        start, size = pieces[p]
        part1[:, start:start + size] = load(p, c0) + in1[:, start:start + size].astype(F32)
        out2[:, start:start + size] = part1[pl.ds(x1, quarter), start:start + size].astype(BF)
        return send(cols(out2, p), cols(in2, p), other_x)

    def step3(p):
        start, size = pieces[p]
        part2[:, start:start + size] = (
            part1[pl.ds(x0, quarter), start:start + size] + in2[:, start:start + size].astype(F32))
        out3[:, start:start + size] = part2[:, start:start + size].astype(BF)
        copies = []
        for k in (1, 2, 3):
            to = pl.multiple_of(lax.rem(z + k, 4) * mine, mine)
            copies.append(send(out3.at[pl.ds(to, mine), start:start + size],
                               in3.at[k - 1, :, start:start + size], others_z[k - 1]))
        return copies

    home = pl.multiple_of(c0 + x0 + z0, mine)
    home_x = pl.multiple_of(c0 + x0, quarter)

    def step4(p):
        start, size = pieces[p]
        total = part2[pl.ds(z0, mine), start:start + size]
        for k in range(3):
            total = total + in3[k, :, start:start + size].astype(F32)
        res[pl.ds(home, mine), start:start + size] = total.astype(BF)
        spot = res.at[pl.ds(home, mine), start:start + size]
        return [send(spot, spot, others_z[k]) for k in range(3)]

    def step5(p):
        start, size = pieces[p]
        spot = res.at[pl.ds(home_x, quarter), start:start + size]
        return send(spot, spot, other_x)

    def step6(p):
        start, size = pieces[p]
        spot = res.at[pl.ds(c0, half), start:start + size]
        return send(spot, spot, other_core)

    def arrived(copies):
        for copy in copies if isinstance(copies, list) else [copies]:
            copy.wait()

    eout[0] = err[...]
    flying = [step1(0), step1(1)]
    error = send(eout.at[0], ein.at[0], other_core)
    for number, step in enumerate((step2, step3, step4, step5, step6)):
        for p in range(2):
            arrived(flying[p])
            flying[p] = step(p)
        if number == 0:
            error.wait()
            eout[1] = eout[0] + ein[0]
            error = send(eout.at[1], ein.at[1], other_x)
        elif number == 1:
            error.wait()
            ez[z] = eout[1] + ein[1]
            error = [send(ez.at[z], ez.at[z], peer) for peer in others_z]
        elif number == 2:
            arrived(error)
            oe[...] = ez[0] + ez[1] + ez[2] + ez[3]

    arrived(flying[0])
    o2[...] = res[:, 0:wide].astype(F32)
    arrived(flying[1])
    o1[...] = res[:, wide:2 * wide].astype(F32)
    oh[...] = res[:, 2 * wide:].astype(F32).T


def summed(g1, g2, gh, err):
    ch, wide = g1.shape
    every = 2 * wide + 128
    vmem = pl.BlockSpec(memory_space=pltpu.VMEM)
    return pl.pallas_call(
        total_kernel,
        out_shape=[
            jax.ShapeDtypeStruct((ch, wide), F32),
            jax.ShapeDtypeStruct((ch, wide), F32),
            jax.ShapeDtypeStruct((128, ch), F32),
            jax.ShapeDtypeStruct(err.shape, F32),
        ],
        in_specs=[vmem] * 4,
        out_specs=[vmem] * 4,
        scratch_shapes=[
            pltpu.VMEM((128, every), BF), pltpu.VMEM((128, every), BF), pltpu.VMEM((128, every), F32),
            pltpu.VMEM((64, every), BF), pltpu.VMEM((64, every), BF), pltpu.VMEM((64, every), F32),
            pltpu.VMEM((3, 16, every), BF), pltpu.VMEM((64, every), BF), pltpu.VMEM((ch, every), BF),
            pltpu.VMEM((2,) + err.shape, F32), pltpu.VMEM((2,) + err.shape, F32),
            pltpu.VMEM((4,) + err.shape, F32),
            pltpu.SemaphoreType.DMA((25,)), pltpu.SemaphoreType.DMA((25,)),
        ],
        compiler_params=pltpu.CompilerParams(
            collective_id=1, has_side_effects=True, vmem_limit_bytes=32 * 2**20),
    )(g1, g2, gh, err)


def around(cells, dim, width):
    count = lax.axis_size("tm")
    head = lax.slice_in_dim(cells, 0, width, axis=dim)
    tail = lax.slice_in_dim(cells, cells.shape[dim] - width, cells.shape[dim], axis=dim)
    return (lax.ppermute(tail, "tm", [(i, i + 1) for i in range(count - 1)]),
            lax.ppermute(head, "tm", [(i + 1, i) for i in range(count - 1)]))


def shards(features, segment, w_first, w_second, w_head, targets):
    rows, ch = features.shape
    count = lax.axis_size("tm")
    every = rows * count
    traits = w_head.shape[1]
    tgt, wht = targets.T, w_head.T
    flo, fhi = around(features, 0, HALO)
    slo, shi = around(segment + 1, 0, EDGE)
    tlo, thi = around(tgt, 1, EDGE)
    seg = jnp.concatenate([slo, segment + 1, shi]).reshape(-1, 128)
    hidden, gfeat, g1, g2, gh, err = local(
        features, flo, fhi, seg, tgt, tlo, thi, w_first, w_second, wht, 1.0 / every**0.5)
    if count == 16 and ch == 256:
        g1, g2, ght, err = summed(g1, g2, gh, err)
    else:
        g1, g2, gh, err = lax.psum((g1, g2, gh, err), "tm")
        ght = gh.T
    loss = jnp.reshape(jnp.sum(err) / (every * traits), (1,))

    def taps(g):
        return jnp.concatenate([g[:, k * ch:(k + 1) * ch] for k in range(3)], 0)

    return hidden, gfeat, taps(g1), taps(g2), ght[:traits].T, loss


def solution(mesh):
    return jax.shard_map(
        shards,
        mesh=mesh,
        in_specs=(
            P(("groups", "tm"), None),
            P(("groups", "tm")),
            P(),
            P(),
            P(),
            P(("groups", "tm"), None),
        ),
        out_specs=(
            P(("groups", "tm"), None),
            P(("groups", "tm"), None),
            P("groups", None),
            P("groups", None),
            P("groups", None),
            P("groups"),
        ),
        check_vma=False,
    )
```

time: 246 us -> 94.3 us (0.38)
  waiting for transfers between devices: 86.4 us -> 0.19 us
  Pallas kernels: 0 us -> 64.1 us
  blocking collectives: 60.5 us -> 0 us
  other arithmetic: 27.4 us -> 3.8 us
  matrix products: 22.1 us -> 0 us
  between operations: 16.3 us -> 2.55 us
  starting transfers between devices: 27.6 us -> 16.2 us
    psum x1 -> x0, waiting for transfers between devices: 82.8 us -> none  [shards(): lax.psum((grad_first, grad_second, grad_head, error_sum), 'tm')]
    pallas_call x0 -> x2, Pallas kernels: none -> 64.1 us  [the longest x1 32.5 us: summed(): pl.pallas_call(total_kernel, out_shape=[jax.ShapeDtypeStruct((ch, wide),...]
    psum x1 -> x0, blocking collectives: 60.5 us -> none  [shards(): lax.psum((grad_first, grad_second, grad_head, error_sum), 'tm')]
    select_n x4 -> x0, other arithmetic: 26.6 us -> none  [the longest x2 13.6 us: back_stack(): jnp.where(keep, padded[start:start + rows], jnp.zeros((), padded.dtype))]
    dot_general x9 -> x0, matrix products: 22.1 us -> none  [the longest x1 4.38 us: shards(): pre_first = jnp.dot(first_in, w_first, preferred_element_type=jnp.float32)]
    ppermute x10 -> x6, starting transfers between devices: 27.6 us -> 16.2 us  [the longest x3 12.4 us: around(): lax.ppermute(tail, 'tm', [(i, i + 1) for i in range(count - 1)])]
    ppermute x10 -> x6, waiting for transfers between devices: 3.54 us -> 0.19 us  [the longest x3 0.18 us: around(): lax.ppermute(tail, 'tm', [(i, i + 1) for i in range(count - 1)])]
  transfers between devices with their start and end apart: 11 -> 6, of which waited for: 3 -> 1; matrix products, arithmetic and copies ran while one was open for 6% -> 2% of each run, Pallas kernels for 0% -> 0%
where the time goes in v1:
time: 94.3 us; the launch traced here: 93.7 us
  Pallas kernels  64.1 us (68%)
  starting transfers between devices  16.2 us (17%)
  local copies, waits for them, and re-layouts  6.81 us (7%)
  other arithmetic  3.8 us (4%)
  between operations  2.55 us (3%)
    pallas_call x1, Pallas kernels, summed(): pl.pallas_call(total_kernel, out_shape=[jax.ShapeDtypeStruct((ch, wide),...  32.5 us
    pallas_call x1, Pallas kernels, local(): pl.pallas_call(functools.partial(compute, rows, scale), out_shape=[jax.Sh...  31.7 us
    ppermute x3, starting transfers between devices, around(): lax.ppermute(tail, 'tm', [(i, i + 1) for i in range(count - 1)])  12.4 us
    unnamed x16, local copies, waits for them, and re-layouts  4.5 us
    ppermute x3, starting transfers between devices, around(): lax.ppermute(head, 'tm', [(i + 1, i) for i in range(count - 1)])  3.85 us
  transfers between devices with their start and end apart: 6, of which 1 were waited for; matrix products, arithmetic and copies ran while one was open for 2% of the time, Pallas kernels for 0%

profile of v1, /device:TPU:0, one launch (start us, length us, event | category | flops | bytes accessed | tf_op | source)
XLA Modules:
  0.0 93.7 jit_solution(9965159528687027610)
XLA Ops:
  0.6 0.7 broadcast_add_fusion
  1.4 2.3 %collective-permute-start.2 = (s32[128]{0:T(128)S(1)}, s32[128]{0:T(128)S(1)}, u32[]{:S(2)}, u32[]{:S(2)}) collective-permute-start(s32[128]{0:T(128)S(1)} %get-tuple-element.36), channel_id=1, source_target_pairs={{0,1},{1,2},{2,3},{3,4},{4,5},{5,6},{6,7},{7,8},{8,9},{9,10},{10,1... | collective-permute-start | bytes 1544 | tf_op jit(solution)/shard_map/ppermute | solution.py:362
  3.7 1.3 %collective-permute-start.3 = (s32[128]{0:T(128)S(1)}, s32[128]{0:T(128)S(1)}, u32[]{:S(2)}, u32[]{:S(2)}) collective-permute-start(s32[128]{0:T(128)S(1)} %get-tuple-element.37), channel_id=1, source_target_pairs={{1,0},{2,1},{3,2},{4,3},{5,4},{6,5},{7,6},{8,7},{9,8},{10,9},{11,1... | collective-permute-start | bytes 1544 | tf_op jit(solution)/shard_map/ppermute | solution.py:363
  5.0 0.7 fusion.3
  5.8 1.3 %collective-permute-start.5 = (f32[32,128]{1,0:T(8,128)S(1)}, f32[32,128]{1,0:T(8,128)S(1)}, u32[]{:S(2)}, u32[]{:S(2)}) collective-permute-start(f32[32,128]{1,0:T(8,128)S(1)} %get-tuple-element.34), channel_id=1, source_target_pairs={{1,0},{2,1},{3,2},{4,3},{5,4},{6,5},{7,6},{8,7},{9,8},{10,9},{11,1... | collective-permute-start | bytes 49160 | tf_op jit(solution)/shard_map/ppermute | solution.py:363
  7.0 5.8 %collective-permute-start.4 = (f32[32,128]{1,0:T(8,128)S(1)}, f32[32,128]{1,0:T(8,128)S(1)}, u32[]{:S(2)}, u32[]{:S(2)}) collective-permute-start(f32[32,128]{1,0:T(8,128)S(1)} %get-tuple-element.35), channel_id=1, source_target_pairs={{0,1},{1,2},{2,3},{3,4},{4,5},{5,6},{6,7},{7,8},{8,9},{9,10},{10,1... | collective-permute-start | bytes 49160 | tf_op jit(solution)/shard_map/ppermute | solution.py:362
  12.8 0.8 fusion
  13.6 1.3 %collective-permute-start.1 = (bf16[64,256]{1,0:T(8,128)(2,1)S(1)}, bf16[64,256]{1,0:T(8,128)(2,1)S(1)}, u32[]{:S(2)}, u32[]{:S(2)}) collective-permute-start(bf16[64,256]{1,0:T(8,128)(2,1)S(1)} %get-tuple-element.26), channel_id=1, source_target_pairs={{1,0},{2,1},{3,2},{4,3},{5,4},{6,5},{7,6},{8,7},{9,8},{10,9},{11,1... | collective-permute-start | bytes 98312 | tf_op jit(solution)/shard_map/ppermute | solution.py:363
  14.9 0.0 collective-permute-done.2
  14.9 4.3 %collective-permute-start = (bf16[64,256]{1,0:T(8,128)(2,1)S(1)}, bf16[64,256]{1,0:T(8,128)(2,1)S(1)}, u32[]{:S(2)}, u32[]{:S(2)}) collective-permute-start(bf16[64,256]{1,0:T(8,128)(2,1)S(1)} %get-tuple-element.27), channel_id=1, source_target_pairs={{0,1},{1,2},{2,3},{3,4},{4,5},{5,6},{6,7},{7,8},{8,9},{9,10},{10,1... | collective-permute-start | bytes 98312 | tf_op jit(solution)/shard_map/ppermute | solution.py:362
  19.2 0.0 collective-permute-done.3
  19.2 0.6 add_bitcast_fusion.seg
  19.8 0.0 collective-permute-done.5.thi
  19.8 0.0 copy-start.6
  19.8 0.0 collective-permute-done.4.tlo
  19.8 0.0 copy-start.7
  19.8 0.0 collective-permute-done.1.fhi
  19.8 0.0 copy-start.4
  19.8 0.2 collective-permute-done.flo
  20.0 0.0 copy-start.5
  20.0 0.4 copy-done.6
  20.4 0.0 copy-done.7
  20.4 0.0 copy-done.4
  20.4 0.2 copy-done.5
  20.6 31.7 %shard_map.109 = (bf16[4096,256]{1,0:T(8,128)(2,1)}, bf16[4096,256]{1,0:T(8,128)(2,1)}, f32[256,768]{1,0:T(8,128)}, f32[256,768]{1,0:T(8,128)}, f32[256,128]{1,0:T(8,128)}, /*index=5*/f32[32,128]{1,0:T(8,128)}) custom-call(bf16[4096,256]{1,0:T(8,128)(2,1)} %feat.1, bf16[64,256]{1,0:T(8,128)(2,1)} %copy-done.5, bf16[64,256]{1,0:T(8,128)(2,1)} %copy-done.4, ...), custom_call_target="tpu_custom_call" | custom-call | flops 10737418240 | bytes 8388608 | tf_op jit(solution)/shard_map/pallas_call | solution.py:176
  52.3 0.0 copy-start
  52.3 1.1 %copy-done = f32[256,768]{1,0:T(8,128)S(1)} copy-done((f32[256,768]{1,0:T(8,128)S(1)}, f32[256,768]{1,0:T(8,128)}, u32[]{:S(2)}) %copy-start) | copy-done | bytes 786456
  53.4 0.0 copy-start.1
  53.4 1.1 %copy-done.1 = f32[256,768]{1,0:T(8,128)S(1)} copy-done((f32[256,768]{1,0:T(8,128)S(1)}, f32[256,768]{1,0:T(8,128)}, u32[]{:S(2)}) %copy-start.1) | copy-done | bytes 786456
  54.6 0.0 copy-start.2
  54.6 0.9 copy-done.2
  55.5 0.0 copy-start.3
  55.5 0.7 copy-done.3
  56.2 32.5 %shard_map.110 = (f32[256,768]{1,0:T(8,128)S(1)}, f32[256,768]{1,0:T(8,128)S(1)}, f32[128,256]{1,0:T(8,128)S(1)}, f32[32,128]{1,0:T(8,128)S(1)}) custom-call(f32[256,768]{1,0:T(8,128)S(1)} %copy-done, f32[256,768]{1,0:T(8,128)S(1)} %copy-done.1, f32[256,128]{1,0:T(8,128)S(1)} %copy-done.2, f32[32,128]{1,0:T(8,128)S(1)} %copy-done.3), custom_call_target="tpu_custom_call" | custom-call | tf_op jit(solution)/shard_map/pallas_call | solution.py:335
  88.7 0.6 slice_bitcast_fusion
  89.3 0.6 reduce_sum.9
  90.5 0.2 fusion.1
  90.7 0.9 pad_maximum_fusion.1
  91.6 0.9 pad_maximum_fusion
  (1 shorter events, 0.0 us)
Async XLA Ops:
  1.4 13.5 %collective-permute-start.2 = (s32[128]{0:T(128)S(1)}, s32[128]{0:T(128)S(1)}, u32[]{:S(2)}, u32[]{:S(2)}) collective-permute-start(s32[128]{0:T(128)S(1)} %get-tuple-element.36), channel_id=1, source_target_pairs={{0,1},{1,2},{2,3},{3,4},{4,5},{5,6},{6,7},{7,8},{8,9},{9,10},{10,1... | collective-permute-start | bytes 1544 | tf_op jit(solution)/shard_map/ppermute | solution.py:362
  3.7 15.5 %collective-permute-start.3 = (s32[128]{0:T(128)S(1)}, s32[128]{0:T(128)S(1)}, u32[]{:S(2)}, u32[]{:S(2)}) collective-permute-start(s32[128]{0:T(128)S(1)} %get-tuple-element.37), channel_id=1, source_target_pairs={{1,0},{2,1},{3,2},{4,3},{5,4},{6,5},{7,6},{8,7},{9,8},{10,9},{11,1... | collective-permute-start | bytes 1544 | tf_op jit(solution)/shard_map/ppermute | solution.py:363
  5.8 14.0 %collective-permute-start.5 = (f32[32,128]{1,0:T(8,128)S(1)}, f32[32,128]{1,0:T(8,128)S(1)}, u32[]{:S(2)}, u32[]{:S(2)}) collective-permute-start(f32[32,128]{1,0:T(8,128)S(1)} %get-tuple-element.34), channel_id=1, source_target_pairs={{1,0},{2,1},{3,2},{4,3},{5,4},{6,5},{7,6},{8,7},{9,8},{10,9},{11,1... | collective-permute-start | bytes 49160 | tf_op jit(solution)/shard_map/ppermute | solution.py:363
  7.0 12.8 %collective-permute-start.4 = (f32[32,128]{1,0:T(8,128)S(1)}, f32[32,128]{1,0:T(8,128)S(1)}, u32[]{:S(2)}, u32[]{:S(2)}) collective-permute-start(f32[32,128]{1,0:T(8,128)S(1)} %get-tuple-element.35), channel_id=1, source_target_pairs={{0,1},{1,2},{2,3},{3,4},{4,5},{5,6},{6,7},{7,8},{8,9},{9,10},{10,1... | collective-permute-start | bytes 49160 | tf_op jit(solution)/shard_map/ppermute | solution.py:362
  13.6 6.2 %collective-permute-start.1 = (bf16[64,256]{1,0:T(8,128)(2,1)S(1)}, bf16[64,256]{1,0:T(8,128)(2,1)S(1)}, u32[]{:S(2)}, u32[]{:S(2)}) collective-permute-start(bf16[64,256]{1,0:T(8,128)(2,1)S(1)} %get-tuple-element.26), channel_id=1, source_target_pairs={{1,0},{2,1},{3,2},{4,3},{5,4},{6,5},{7,6},{8,7},{9,8},{10,9},{11,1... | collective-permute-start | bytes 98312 | tf_op jit(solution)/shard_map/ppermute | solution.py:363
  14.9 5.1 %collective-permute-start = (bf16[64,256]{1,0:T(8,128)(2,1)S(1)}, bf16[64,256]{1,0:T(8,128)(2,1)S(1)}, u32[]{:S(2)}, u32[]{:S(2)}) collective-permute-start(bf16[64,256]{1,0:T(8,128)(2,1)S(1)} %get-tuple-element.27), channel_id=1, source_target_pairs={{0,1},{1,2},{2,3},{3,4},{4,5},{5,6},{6,7},{7,8},{8,9},{9,10},{10,1... | collective-permute-start | bytes 98312 | tf_op jit(solution)/shard_map/ppermute | solution.py:362
  19.8 0.6 copy-start.6
  19.8 0.6 copy-start.7
  19.8 0.6 copy-start.4
  20.0 0.6 copy-start.5
  52.3 1.1 %copy-start = (f32[256,768]{1,0:T(8,128)S(1)}, f32[256,768]{1,0:T(8,128)}, u32[]{:S(2)}) copy-start(f32[256,768]{1,0:T(8,128)} %get-tuple-element.18.g1) | copy-start | bytes 2359300
  53.4 1.1 %copy-start.1 = (f32[256,768]{1,0:T(8,128)S(1)}, f32[256,768]{1,0:T(8,128)}, u32[]{:S(2)}) copy-start(f32[256,768]{1,0:T(8,128)} %get-tuple-element.19.g2) | copy-start | bytes 2359300
  54.6 0.9 copy-start.2
  55.5 0.7 copy-start.3

commit v2 on v1

--- a/solution.py
+++ b/solution.py
@@ -23,7 +23,7 @@
 
 def compute(rows, scale, feat, flo, fhi, seg, tgt, tlo, thi, w1, w2, wht,
             hid, gfeat, g1, g2, gh, err,
-            fb, f32, segc, msk, act, gp2, gp1, ghid, w1t, w2t, ght, sem):
+            fb, f32, segc, msk, act, gp2, gp1, ghid, w1t, w2t, ght, hids, gfs, sem):
     ch = w1.shape[1]
     total = rows + 2 * BASE
     step = min(512, rows)
@@ -130,7 +130,8 @@
 
     def middle(t, q):
         h, error, gout, back = second(q, step, tgt[:, pl.ds(t, step)])
-        hid[pl.ds(t, step), :] = h
+        hids[pl.ds(t, step), :] = h
+        pltpu.make_async_copy(hids.at[pl.ds(t, step)], hid.at[pl.ds(t, step)], sem.at[3]).start()
         ghid[pl.ds(t, step), :] = back
         square = error * error
         part = square[:, 0:128]
@@ -160,10 +161,13 @@
     def final(t, q):
         b = near(gp1, gp1[pl.ds(q, step), :].astype(BF), q, step, True)
         g1[...] += dot(fb[pl.ds(q, step), :], b, 0, 0)
-        gfeat[pl.ds(t, step), :] = (ghid[pl.ds(t, step), :] + dot(b, w1t[...])).astype(BF)
+        gfs[pl.ds(t, step), :] = (ghid[pl.ds(t, step), :] + dot(b, w1t[...])).astype(BF)
+        pltpu.make_async_copy(gfs.at[pl.ds(t, step)], gfeat.at[pl.ds(t, step)], sem.at[4]).start()
 
     loop(final)
     gh[...] = ght[...].T
+    pltpu.make_async_copy(hids, hid, sem.at[3]).wait()
+    pltpu.make_async_copy(gfs, gfeat, sem.at[4]).wait()
 
 
 def local(features, flo, fhi, seg, tgt, tlo, thi, w_first, w_second, wht, scale):
@@ -184,7 +188,7 @@
             jax.ShapeDtypeStruct((traits, 128), F32),
         ],
         in_specs=[anys] * 3 + [vmem] * 7,
-        out_specs=[vmem] * 6,
+        out_specs=[pl.BlockSpec(memory_space=pltpu.HBM)] * 2 + [vmem] * 4,
         scratch_shapes=[
             pltpu.VMEM((total, ch), BF),
             pltpu.VMEM((total, ch), F32),
@@ -197,14 +201,16 @@
             pltpu.VMEM((3 * ch, ch), BF),
             pltpu.VMEM((3 * ch, ch), BF),
             pltpu.VMEM((128, ch), F32),
-            pltpu.SemaphoreType.DMA((3,)),
+            pltpu.VMEM((rows, ch), BF),
+            pltpu.VMEM((rows, ch), BF),
+            pltpu.SemaphoreType.DMA((5,)),
         ],
         compiler_params=pltpu.CompilerParams(vmem_limit_bytes=56 * 2**20),
         cost_estimate=pl.CostEstimate(flops=flops, bytes_accessed=8 * rows * ch, transcendentals=0),
     )(features, flo, fhi, seg, tgt, tlo, thi, w_first, w_second, wht)
 
 
-def total_kernel(g1, g2, gh, err, o1, o2, oh, oe,
+def total_kernel(h1, h2, hh, he, o1, o2, oh, oe, g1, g2, gh, err, lsem,
                  out1, in1, part1, out2, in2, part2, in3, out3, res, eout, ein, ez, ssem, rsem):
     me = lax.axis_index("tm")
     group = lax.axis_index("groups")
@@ -217,6 +223,10 @@
     other_x = at(z, 1 - x, core)
     others_z = [at(lax.rem(z + k, 4), x, core) for k in (1, 2, 3)]
 
+    fetched = [pltpu.make_async_copy(src, dst, lsem.at[n])
+               for n, (src, dst) in enumerate(((h2, g2), (h1, g1), (hh, gh), (he, err)))]
+    for copy in fetched:
+        copy.start()
     barrier = pltpu.get_barrier_semaphore()
     for peer in [other_core, other_x] + others_z:
         pl.semaphore_signal(barrier, inc=1, device_id=peer, device_id_type=MESH)
@@ -233,7 +243,6 @@
         copy.start()
         return copy
 
-    sent = []
     wide = g2.shape[1]
     half, quarter, mine = 128, 64, 16
     c0 = pl.multiple_of(core * half, half)
@@ -242,12 +251,13 @@
     x1 = pl.multiple_of((1 - x) * quarter, quarter)
     z0 = pl.multiple_of(z * mine, mine)
 
-    pieces = [(0, wide), (wide, wide + 128)]
+    part = wide // 2
+    pieces = [(0, part), (part, part), (wide, part), (wide + part, part + 128)]
 
     def load(piece, start):
-        if piece == 0:
-            return g2[pl.ds(start, half), :]
-        return jnp.concatenate([g1[pl.ds(start, half), :], gh[pl.ds(start, half), :]], 1)
+        left = (piece % 2) * part
+        own = (g2 if piece < 2 else g1)[pl.ds(start, half), left:left + part]
+        return own if piece < 3 else jnp.concatenate([own, gh[pl.ds(start, half), :]], 1)
 
     def cols(ref, piece):
         start, size = pieces[piece]
@@ -302,11 +312,15 @@
         for copy in copies if isinstance(copies, list) else [copies]:
             copy.wait()
 
+    fetched[0].wait()
+    flying = [step1(0), step1(1)]
+    for copy in fetched[1:]:
+        copy.wait()
+    flying += [step1(2), step1(3)]
     eout[0] = err[...]
-    flying = [step1(0), step1(1)]
     error = send(eout.at[0], ein.at[0], other_core)
     for number, step in enumerate((step2, step3, step4, step5, step6)):
-        for p in range(2):
+        for p in range(4):
             arrived(flying[p])
             flying[p] = step(p)
         if number == 0:
@@ -321,10 +335,10 @@
             arrived(error)
             oe[...] = ez[0] + ez[1] + ez[2] + ez[3]
 
-    arrived(flying[0])
-    o2[...] = res[:, 0:wide].astype(F32)
-    arrived(flying[1])
-    o1[...] = res[:, wide:2 * wide].astype(F32)
+    for p in range(4):
+        arrived(flying[p])
+        left = (p % 2) * part
+        (o2 if p < 2 else o1)[:, left:left + part] = res[:, p * part:(p + 1) * part].astype(F32)
     oh[...] = res[:, 2 * wide:].astype(F32).T
 
 
@@ -340,27 +354,75 @@
             jax.ShapeDtypeStruct((128, ch), F32),
             jax.ShapeDtypeStruct(err.shape, F32),
         ],
-        in_specs=[vmem] * 4,
+        in_specs=[pl.BlockSpec(memory_space=pltpu.HBM)] * 4,
         out_specs=[vmem] * 4,
         scratch_shapes=[
+            pltpu.VMEM((ch, wide), F32), pltpu.VMEM((ch, wide), F32), pltpu.VMEM((ch, 128), F32),
+            pltpu.VMEM(err.shape, F32), pltpu.SemaphoreType.DMA((4,)),
             pltpu.VMEM((128, every), BF), pltpu.VMEM((128, every), BF), pltpu.VMEM((128, every), F32),
             pltpu.VMEM((64, every), BF), pltpu.VMEM((64, every), BF), pltpu.VMEM((64, every), F32),
             pltpu.VMEM((3, 16, every), BF), pltpu.VMEM((64, every), BF), pltpu.VMEM((ch, every), BF),
             pltpu.VMEM((2,) + err.shape, F32), pltpu.VMEM((2,) + err.shape, F32),
             pltpu.VMEM((4,) + err.shape, F32),
-            pltpu.SemaphoreType.DMA((25,)), pltpu.SemaphoreType.DMA((25,)),
+            pltpu.SemaphoreType.DMA((45,)), pltpu.SemaphoreType.DMA((45,)),
         ],
         compiler_params=pltpu.CompilerParams(
             collective_id=1, has_side_effects=True, vmem_limit_bytes=32 * 2**20),
     )(g1, g2, gh, err)
 
 
-def around(cells, dim, width):
-    count = lax.axis_size("tm")
-    head = lax.slice_in_dim(cells, 0, width, axis=dim)
-    tail = lax.slice_in_dim(cells, cells.shape[dim] - width, cells.shape[dim], axis=dim)
-    return (lax.ppermute(tail, "tm", [(i, i + 1) for i in range(count - 1)]),
-            lax.ppermute(head, "tm", [(i + 1, i) for i in range(count - 1)]))
+def halo_kernel(count, feat, seg, tgt, flo, fhi, tlo, thi, both, inlo, inhi, tinlo, tinhi, slo, shi, ssem, rsem):
+    me = lax.axis_index("tm")
+    group = lax.axis_index("groups")
+    right = (group, lax.rem(me + 1, count))
+    left = (group, lax.rem(me + count - 1, count))
+    barrier = pltpu.get_barrier_semaphore()
+    for peer in (left, right):
+        pl.semaphore_signal(barrier, inc=1, device_id=peer, device_id_type=MESH)
+    pl.semaphore_wait(barrier, 2)
+    rows, lines = feat.shape[0], seg.shape[0]
+    plan = [
+        (feat.at[pl.ds(rows - HALO, HALO)], inlo, right),
+        (feat.at[pl.ds(0, HALO)], inhi, left),
+        (tgt.at[:, pl.ds(rows - EDGE, EDGE)], tinlo, right),
+        (tgt.at[:, pl.ds(0, EDGE)], tinhi, left),
+        (seg.at[pl.ds(lines - 8, 8)], slo, right),
+        (seg.at[pl.ds(0, 8)], shi, left),
+    ]
+    copies = [
+        pltpu.make_async_remote_copy(
+            src_ref=src, dst_ref=dst, send_sem=ssem.at[n], recv_sem=rsem.at[n],
+            device_id=peer, device_id_type=MESH)
+        for n, (src, dst, peer) in enumerate(plan)
+    ]
+    for copy in copies:
+        copy.start()
+    both[1:1 + lines, :] = seg[...] + 1
+    for copy in copies:
+        copy.wait()
+    flo[...] = inlo[...]
+    fhi[...] = inhi[...]
+    tlo[...] = tinlo[...]
+    thi[...] = tinhi[...]
+    both[0:1, :] = jnp.where(me == 0, 0, slo[7:8, :] + 1)
+    both[1 + lines:2 + lines, :] = jnp.where(me == count - 1, 0, shi[0:1, :] + 1)
+
+
+def halos(features, segment, tgt):
+    ch, traits = features.shape[1], tgt.shape[0]
+    lines = segment.shape[0] // 128
+    vmem = pl.BlockSpec(memory_space=pltpu.VMEM)
+    hbm = pl.BlockSpec(memory_space=pltpu.HBM)
+    shapes = [((HALO, ch), BF)] * 2 + [((traits, EDGE), F32)] * 2
+    return pl.pallas_call(
+        functools.partial(halo_kernel, lax.axis_size("tm")),
+        out_shape=[jax.ShapeDtypeStruct(*s) for s in shapes + [((lines + 2, 128), jnp.int32)]],
+        in_specs=[hbm, vmem, hbm],
+        out_specs=[vmem] * 5,
+        scratch_shapes=[pltpu.VMEM(*s) for s in shapes + [((8, 128), jnp.int32)] * 2] + [
+            pltpu.SemaphoreType.DMA((6,)), pltpu.SemaphoreType.DMA((6,))],
+        compiler_params=pltpu.CompilerParams(collective_id=2, has_side_effects=True),
+    )(features, segment.reshape(-1, 128), tgt)
 
 
 def shards(features, segment, w_first, w_second, w_head, targets):
@@ -369,10 +431,7 @@
     every = rows * count
     traits = w_head.shape[1]
     tgt, wht = targets.T, w_head.T
-    flo, fhi = around(features, 0, HALO)
-    slo, shi = around(segment + 1, 0, EDGE)
-    tlo, thi = around(tgt, 1, EDGE)
-    seg = jnp.concatenate([slo, segment + 1, shi]).reshape(-1, 128)
+    flo, fhi, tlo, thi, seg = halos(features, segment, tgt)
     hidden, gfeat, g1, g2, gh, err = local(
         features, flo, fhi, seg, tgt, tlo, thi, w_first, w_second, wht, 1.0 / every**0.5)
     if count == 16 and ch == 256:

time: 94.3 us -> 76.7 us (0.81)
  starting transfers between devices: 16.2 us -> 0 us
  Pallas kernels: 64.1 us -> 66.7 us
  local copies, waits for them, and re-layouts: 6.81 us -> 4.66 us
  other arithmetic: 3.8 us -> 2.47 us
    ppermute x6 -> x0, starting transfers between devices: 16.2 us -> none  [the longest x3 12.4 us: around(): lax.ppermute(tail, 'tm', [(i, i + 1) for i in range(count - 1)])]
    pallas_call x0 -> x1, Pallas kernels: none -> 9.61 us  [halos(): pl.pallas_call(functools.partial(halo_kernel, lax.axis_size('tm')), out_s...]
    pallas_call x1, Pallas kernels: 32.5 us -> 25.5 us  [summed(): pl.pallas_call(total_kernel, out_shape=[jax.ShapeDtypeStruct((ch, wide),...]
    slice x3 -> x0, local copies, waits for them, and re-layouts: 1.53 us -> none  [the longest x2 1.52 us: around(): head = lax.slice_in_dim(cells, 0, width, axis=dim)]
    unnamed x16 -> x8, local copies, waits for them, and re-layouts: 4.5 us -> 3.88 us
  transfers between devices with their start and end apart: 6 -> 0, of which waited for: 1 -> 0; matrix products, arithmetic and copies ran while one was open for 2% -> 0% of each run, Pallas kernels for 0% -> 0%
where the time goes in v2:
time: 76.7 us; the launch traced here: 76.3 us
  Pallas kernels  66.7 us (87%)
  local copies, waits for them, and re-layouts  4.66 us (6%)
  other arithmetic  2.47 us (3%)
  between operations  2.46 us (3%)
    pallas_call x1, Pallas kernels, local(): pl.pallas_call(functools.partial(compute, rows, scale), out_shape=[jax.Sh...  31.6 us
    pallas_call x1, Pallas kernels, summed(): pl.pallas_call(total_kernel, out_shape=[jax.ShapeDtypeStruct((ch, wide),...  25.5 us
    pallas_call x1, Pallas kernels, halos(): pl.pallas_call(functools.partial(halo_kernel, lax.axis_size('tm')), out_s...  9.61 us
    unnamed x8, local copies, waits for them, and re-layouts  3.88 us
    concatenate x2, other arithmetic, taps(): return jnp.concatenate([g[:, k * ch:(k + 1) * ch] for k in range(3)], 0)  1.87 us

profile of v2, /device:TPU:0, one launch (start us, length us, event | category | flops | bytes accessed | tf_op | source)
XLA Modules:
  0.0 76.3 jit_solution(7000353407505656928)
XLA Ops:
  0.6 9.6 %shard_map.109 = (bf16[64,256]{1,0:T(8,128)(2,1)}, bf16[64,256]{1,0:T(8,128)(2,1)}, f32[32,128]{1,0:T(8,128)}, f32[32,128]{1,0:T(8,128)}, s32[34,128]{1,0:T(8,128)}) custom-call(bf16[4096,256]{1,0:T(8,128)(2,1)} %feat.3, s32[32,128]{1,0:T(8,128)} %bitcast.8, f32[32,4096]{1,0:T(8,128)} %bitcast.6), custom_call_target="tpu_custom_call" | custom-call | tf_op jit(solution)/shard_map/pallas_call | solution.py:417
  10.2 31.6 %shard_map.110 = (bf16[4096,256]{1,0:T(8,128)(2,1)}, bf16[4096,256]{1,0:T(8,128)(2,1)}, f32[256,768]{1,0:T(8,128)}, f32[256,768]{1,0:T(8,128)}, f32[256,128]{1,0:T(8,128)}, /*index=5*/f32[32,128]{1,0:T(8,128)}) custom-call(bf16[4096,256]{1,0:T(8,128)(2,1)} %feat.3, bf16[64,256]{1,0:T(8,128)(2,1)} %get-tuple-element.21.flo, ...), custom_call_target="tpu_custom_call" | custom-call | flops 10737418240 | bytes 8388608 | tf_op jit(solution)/shard_map/pallas_call | solution.py:180
  41.9 0.0 copy-start
  41.9 1.1 %copy-done = f32[256,768]{1,0:T(8,128)S(1)} copy-done((f32[256,768]{1,0:T(8,128)S(1)}, f32[256,768]{1,0:T(8,128)}, u32[]{:S(2)}) %copy-start) | copy-done | bytes 786456
  43.0 0.0 copy-start.1
  43.0 1.1 %copy-done.1 = f32[256,768]{1,0:T(8,128)S(1)} copy-done((f32[256,768]{1,0:T(8,128)S(1)}, f32[256,768]{1,0:T(8,128)}, u32[]{:S(2)}) %copy-start.1) | copy-done | bytes 786456
  44.2 0.0 copy-start.2
  44.2 0.9 %copy-done.2 = f32[256,128]{1,0:T(8,128)S(1)} copy-done((f32[256,128]{1,0:T(8,128)S(1)}, f32[256,128]{1,0:T(8,128)}, u32[]{:S(2)}) %copy-start.2) | copy-done | bytes 131096
  45.1 0.0 copy-start.3
  45.1 0.7 copy-done.3
  45.8 25.5 %shard_map.111 = (f32[256,768]{1,0:T(8,128)S(1)}, f32[256,768]{1,0:T(8,128)S(1)}, f32[128,256]{1,0:T(8,128)S(1)}, f32[32,128]{1,0:T(8,128)S(1)}) custom-call(f32[256,768]{1,0:T(8,128)S(1)} %copy-done, f32[256,768]{1,0:T(8,128)S(1)} %copy-done.1, f32[256,128]{1,0:T(8,128)S(1)} %copy-done.2, f32[32,128]{1,0:T(8,128)S(1)} %copy-done.3), custom_call_target="tpu_custom_call" | custom-call | tf_op jit(solution)/shard_map/pallas_call | solution.py:349
  71.3 0.6 reduce_sum.9
  72.5 0.2 fusion
  72.7 0.9 %pad_maximum_fusion.1 = f32[768,256]{1,0:T(8,128)} fusion(f32[256,256]{1,0:T(8,128)S(1)} %get-tuple-element.37, f32[256,256]{1,0:T(8,128)S(1)} %get-tuple-element.38, f32[256,256]{1,0:T(8,128)S(1)} %get-tuple-element.36), kind=kLoop, calls=%fused_computation.1 | loop fusion | flops 393216 | bytes 1572864 | tf_op jit(solution)/shard_map/concatenate | solution.py:445
  73.7 0.6 slice_bitcast_fusion
  74.3 0.9 %pad_maximum_fusion = f32[768,256]{1,0:T(8,128)} fusion(f32[256,256]{1,0:T(8,128)S(1)} %get-tuple-element.43, f32[256,256]{1,0:T(8,128)S(1)} %get-tuple-element.42, f32[256,256]{1,0:T(8,128)S(1)} %get-tuple-element.44), kind=kLoop, calls=%fused_computation | loop fusion | flops 393216 | bytes 1572864 | tf_op jit(solution)/shard_map/concatenate | solution.py:445
Async XLA Ops:
  41.9 1.1 %copy-start = (f32[256,768]{1,0:T(8,128)S(1)}, f32[256,768]{1,0:T(8,128)}, u32[]{:S(2)}) copy-start(f32[256,768]{1,0:T(8,128)} %get-tuple-element.28.h1) | copy-start | bytes 2359300
  43.0 1.1 %copy-start.1 = (f32[256,768]{1,0:T(8,128)S(1)}, f32[256,768]{1,0:T(8,128)}, u32[]{:S(2)}) copy-start(f32[256,768]{1,0:T(8,128)} %get-tuple-element.29.h2) | copy-start | bytes 2359300
  44.2 0.9 %copy-start.2 = (f32[256,128]{1,0:T(8,128)S(1)}, f32[256,128]{1,0:T(8,128)}, u32[]{:S(2)}) copy-start(f32[256,128]{1,0:T(8,128)} %get-tuple-element.30.hh) | copy-start | bytes 393220
  45.1 0.7 copy-start.3

commit v3 on v2

--- a/solution.py
+++ b/solution.py
@@ -26,7 +26,7 @@
             fb, f32, segc, msk, act, gp2, gp1, ghid, w1t, w2t, ght, hids, gfs, sem):
     ch = w1.shape[1]
     total = rows + 2 * BASE
-    step = min(512, rows)
+    step = min(1024, rows)
     steps = rows // step
 
     copies = [
@@ -42,27 +42,30 @@
     ones = jnp.ones((256, 128), BF)
 
     def column(i, _):
-        row = jnp.broadcast_to(seg[pl.ds(i, 1), :], (128, 128))
+        row = jnp.broadcast_to(seg[i:i + 1, :], (128, 128))
         low = row & 255
         high = row - low
         both = jnp.concatenate([jnp.where(diagonal, low, 0), jnp.where(diagonal, high, 0)], 1)
-        segc[pl.ds(pl.multiple_of(GAP + i * 128, 16), 128), :] = dot(both.astype(F32).astype(BF), ones)
+        segc[pl.ds(GAP + i * 128, 128), :] = dot(both.astype(F32).astype(BF), ones)
         return 0
 
-    lax.fori_loop(0, seg.shape[0], column, 0)
+    for i in range(seg.shape[0]):
+        column(i, 0)
     segc[0:GAP, :] = jnp.full((GAP, 128), -1.0, F32)
     segc[total - GAP:total, :] = jnp.full((GAP, 128), -1.0, F32)
 
+    block = 2 * 128 if seg.shape[0] % 2 == 0 else 128
+
     def masks(i, _):
-        q = pl.multiple_of(GAP + i * 128, 16)
-        around = segc.at[pl.ds(q - GAP, 128 + 2 * GAP), :]
-        center = around[GAP:GAP + 128, :]
+        q = pl.multiple_of(GAP + i * block, 16)
+        around = segc.at[pl.ds(q - GAP, block + 2 * GAP), :]
+        center = around[GAP:GAP + block, :]
         for n, off in enumerate((-D_FIRST, D_FIRST, -D_SECOND, D_SECOND)):
-            same = around[GAP + off:GAP + off + 128, :] == center
-            msk[n, pl.ds(q, 128), :] = jnp.where(same, 1.0, 0.0).astype(BF)
+            same = around[GAP + off:GAP + off + block, :] == center
+            msk[n, pl.ds(q, block), :] = jnp.where(same, 1.0, 0.0).astype(BF)
         return 0
 
-    lax.fori_loop(0, seg.shape[0], masks, 0)
+    lax.fori_loop(0, seg.shape[0] * 128 // block, masks, 0)
 
     for k in range(3):
         w1t[k * ch:(k + 1) * ch, :] = w1[k * ch:(k + 1) * ch, :].T
@@ -205,12 +208,12 @@
             pltpu.VMEM((rows, ch), BF),
             pltpu.SemaphoreType.DMA((5,)),
         ],
-        compiler_params=pltpu.CompilerParams(vmem_limit_bytes=56 * 2**20),
+        compiler_params=pltpu.CompilerParams(vmem_limit_bytes=62 * 2**20),
         cost_estimate=pl.CostEstimate(flops=flops, bytes_accessed=8 * rows * ch, transcendentals=0),
     )(features, flo, fhi, seg, tgt, tlo, thi, w_first, w_second, wht)
 
 
-def total_kernel(h1, h2, hh, he, o1, o2, oh, oe, g1, g2, gh, err, lsem,
+def total_kernel(share, h1, h2, hh, he, o1, o2, oh, oe, g1, g2, gh, err, lsem,
                  out1, in1, part1, out2, in2, part2, in3, out3, res, eout, ein, ez, ssem, rsem):
     me = lax.axis_index("tm")
     group = lax.axis_index("groups")
@@ -333,7 +336,8 @@
             error = [send(ez.at[z], ez.at[z], peer) for peer in others_z]
         elif number == 2:
             arrived(error)
-            oe[...] = ez[0] + ez[1] + ez[2] + ez[3]
+            every = jnp.sum(ez[0] + ez[1] + ez[2] + ez[3], axis=(0, 1), keepdims=True)
+            oe[...] = jnp.broadcast_to(every * share, oe.shape)
 
     for p in range(4):
         arrived(flying[p])
@@ -342,17 +346,17 @@
     oh[...] = res[:, 2 * wide:].astype(F32).T
 
 
-def summed(g1, g2, gh, err):
+def summed(g1, g2, gh, err, share):
     ch, wide = g1.shape
     every = 2 * wide + 128
     vmem = pl.BlockSpec(memory_space=pltpu.VMEM)
     return pl.pallas_call(
-        total_kernel,
+        functools.partial(total_kernel, share),
         out_shape=[
             jax.ShapeDtypeStruct((ch, wide), F32),
             jax.ShapeDtypeStruct((ch, wide), F32),
             jax.ShapeDtypeStruct((128, ch), F32),
-            jax.ShapeDtypeStruct(err.shape, F32),
+            jax.ShapeDtypeStruct((8, 128), F32),
         ],
         in_specs=[pl.BlockSpec(memory_space=pltpu.HBM)] * 4,
         out_specs=[vmem] * 4,
@@ -367,7 +371,7 @@
             pltpu.SemaphoreType.DMA((45,)), pltpu.SemaphoreType.DMA((45,)),
         ],
         compiler_params=pltpu.CompilerParams(
-            collective_id=1, has_side_effects=True, vmem_limit_bytes=32 * 2**20),
+            collective_id=1, has_side_effects=True, vmem_limit_bytes=62 * 2**20),
     )(g1, g2, gh, err)
 
 
@@ -435,11 +439,12 @@
     hidden, gfeat, g1, g2, gh, err = local(
         features, flo, fhi, seg, tgt, tlo, thi, w_first, w_second, wht, 1.0 / every**0.5)
     if count == 16 and ch == 256:
-        g1, g2, ght, err = summed(g1, g2, gh, err)
+        g1, g2, ght, mean = summed(g1, g2, gh, err, 1.0 / (every * traits))
+        loss = mean[0, 0:1]
     else:
         g1, g2, gh, err = lax.psum((g1, g2, gh, err), "tm")
         ght = gh.T
-    loss = jnp.reshape(jnp.sum(err) / (every * traits), (1,))
+        loss = jnp.reshape(jnp.sum(err) / (every * traits), (1,))
 
     def taps(g):
         return jnp.concatenate([g[:, k * ch:(k + 1) * ch] for k in range(3)], 0)

time: 76.7 us -> 66.2 us (0.86)
  Pallas kernels: 66.7 us -> 59.3 us
  between operations: 2.46 us -> 0.66 us
    pallas_call x1, Pallas kernels: 31.6 us -> 23.3 us  [local(): pl.pallas_call(functools.partial(compute, rows, scale), out_shape=[jax.Sh...]
    unnamed x8 -> x0, local copies, waits for them, and re-layouts: 3.88 us -> none
    slice x1, local copies, waits for them, and re-layouts: 0.16 us -> 1.46 us  [taps(): return jnp.concatenate([g[:, k * ch:(k + 1) * ch] for k in range(3)], 0)]
    slice x0 -> x1, local copies, waits for them, and re-layouts: none -> 1.2 us  [shards(): loss = mean[0, 0:1]]
    pallas_call x1, Pallas kernels: 25.5 us -> 26.4 us  [summed(): pl.pallas_call(functools.partial(total_kernel, share), out_shape=[jax.Sha...]
where the time goes in v3:
time: 66.2 us; the launch traced here: 65.9 us
  Pallas kernels  59.3 us (90%)
  local copies, waits for them, and re-layouts  4.03 us (6%)
  other arithmetic  1.86 us (3%)
    pallas_call x1, Pallas kernels, summed(): pl.pallas_call(functools.partial(total_kernel, share), out_shape=[jax.Sha...  26.4 us
    pallas_call x1, Pallas kernels, local(): pl.pallas_call(functools.partial(compute, rows, scale), out_shape=[jax.Sh...  23.3 us
    pallas_call x1, Pallas kernels, halos(): pl.pallas_call(functools.partial(halo_kernel, lax.axis_size('tm')), out_s...  9.61 us
    concatenate x2, other arithmetic, taps(): return jnp.concatenate([g[:, k * ch:(k + 1) * ch] for k in range(3)], 0)  1.86 us
    slice x1, local copies, waits for them, and re-layouts, taps(): return jnp.concatenate([g[:, k * ch:(k + 1) * ch] for k in range(3)], 0)  1.46 us
    transpose x1, local copies, waits for them, and re-layouts, shards(): return (hidden, gfeat, taps(g1), taps(g2), ght[:traits].T, loss)  1.37 us

profile of v3, /device:TPU:0, one launch (start us, length us, event | category | flops | bytes accessed | tf_op | source)
XLA Modules:
  0.0 65.9 jit_solution(13465667872072410716)
XLA Ops:
  0.6 9.6 %shard_map.109 = (bf16[64,256]{1,0:T(8,128)(2,1)}, bf16[64,256]{1,0:T(8,128)(2,1)}, f32[32,128]{1,0:T(8,128)}, f32[32,128]{1,0:T(8,128)}, s32[34,128]{1,0:T(8,128)}) custom-call(bf16[4096,256]{1,0:T(8,128)(2,1)} %feat.3, s32[32,128]{1,0:T(8,128)} %bitcast.8, f32[32,4096]{1,0:T(8,128)} %bitcast.6), custom_call_target="tpu_custom_call" | custom-call | tf_op jit(solution)/shard_map/pallas_call | solution.py:421
  10.2 23.3 %shard_map.110 = (bf16[4096,256]{1,0:T(8,128)(2,1)}, bf16[4096,256]{1,0:T(8,128)(2,1)}, f32[256,768]{1,0:T(8,128)}, f32[256,768]{1,0:T(8,128)}, f32[256,128]{1,0:T(8,128)}, /*index=5*/f32[32,128]{1,0:T(8,128)}) custom-call(bf16[4096,256]{1,0:T(8,128)(2,1)} %feat.3, bf16[64,256]{1,0:T(8,128)(2,1)} %get-tuple-element.21.flo, ...), custom_call_target="tpu_custom_call" | custom-call | flops 10737418240 | bytes 8388608 | tf_op jit(solution)/shard_map/pallas_call | solution.py:183
  33.6 26.4 %shard_map.111 = (f32[256,768]{1,0:T(8,128)}, f32[256,768]{1,0:T(8,128)}, f32[128,256]{1,0:T(8,128)}, f32[8,128]{1,0:T(8,128)}) custom-call(f32[256,768]{1,0:T(8,128)} %get-tuple-element.28.h1, f32[256,768]{1,0:T(8,128)} %get-tuple-element.29.h2, f32[256,128]{1,0:T(8,128)} %get-tuple-element.30.hh, f32[32,128]{1,0:T(8,128)} %get-tuple-element.31.he), custom_call_target="tpu_custom_call" | custom-call | tf_op jit(solution)/shard_map/pallas_call | solution.py:353
  60.0 1.2 %slice.31 = f32[1,1]{1,0:T(1,128)} slice(f32[8,128]{1,0:T(8,128)} %get-tuple-element.35), slice={[0:1], [0:1]} | slice | bytes 8 | tf_op jit(solution)/shard_map/slice | solution.py:443
  61.2 1.5 %fusion = (f32[256,256]{1,0:T(8,128)S(1)}, f32[256,256]{1,0:T(8,128)S(1)}, f32[256,256]{1,0:T(8,128)S(1)}, f32[256,256]{1,0:T(8,128)S(1)}, f32[256,256]{1,0:T(8,128)S(1)}, /*index=5*/f32[256,256]{1,0:T(8,128)S(1)}) fusion(f32[256,768]{1,0:T(8,128)} %get-tuple-element.33, f32[256,768]{1,0:T(8,128)} %get-tuple-element.32), kind=kLoop, calls=%fused_computation.3 | loop fusion | bytes 3145728 | tf_op jit(solution)/shard_map/slice | solution.py:450
  62.6 0.9 %pad_maximum_fusion.1 = f32[768,256]{1,0:T(8,128)} fusion(f32[256,256]{1,0:T(8,128)S(1)} %get-tuple-element.37, f32[256,256]{1,0:T(8,128)S(1)} %get-tuple-element.38, f32[256,256]{1,0:T(8,128)S(1)} %get-tuple-element.36), kind=kLoop, calls=%fused_computation.1 | loop fusion | flops 393216 | bytes 1572864 | tf_op jit(solution)/shard_map/concatenate | solution.py:450
  63.6 1.4 %slice_bitcast_fusion = f32[256,32]{0,1:T(8,128)} fusion(f32[128,256]{1,0:T(8,128)} %get-tuple-element.34), kind=kLoop, calls=%fused_computation.2 | loop fusion | bytes 65536 | tf_op jit(solution)/shard_map/transpose | solution.py:452
  64.9 0.9 %pad_maximum_fusion = f32[768,256]{1,0:T(8,128)} fusion(f32[256,256]{1,0:T(8,128)S(1)} %get-tuple-element.43, f32[256,256]{1,0:T(8,128)S(1)} %get-tuple-element.42, f32[256,256]{1,0:T(8,128)S(1)} %get-tuple-element.44), kind=kLoop, calls=%fused_computation | loop fusion | flops 393216 | bytes 1572864 | tf_op jit(solution)/shard_map/concatenate | solution.py:450

commit v4 on v3

--- a/solution.py
+++ b/solution.py
@@ -213,7 +213,7 @@
     )(features, flo, fhi, seg, tgt, tlo, thi, w_first, w_second, wht)
 
 
-def total_kernel(share, h1, h2, hh, he, o1, o2, oh, oe, g1, g2, gh, err, lsem,
+def total_kernel(share, h1, h2, hh, he, ores, oe, g1, g2, gh, err, lsem,
                  out1, in1, part1, out2, in2, part2, in3, out3, res, eout, ein, ez, ssem, rsem):
     me = lax.axis_index("tm")
     group = lax.axis_index("groups")
@@ -341,9 +341,36 @@
 
     for p in range(4):
         arrived(flying[p])
-        left = (p % 2) * part
-        (o2 if p < 2 else o1)[:, left:left + part] = res[:, p * part:(p + 1) * part].astype(F32)
-    oh[...] = res[:, 2 * wide:].astype(F32).T
+        start, size = pieces[p]
+        ores[:, start:start + size] = res[:, start:start + size]
+
+
+def spread_kernel(sums, mean, first, second, head, loss):
+    ch, wide = sums.shape[0], first.shape[0]
+    for k in range(3):
+        second[k * ch:(k + 1) * ch, :] = sums[:, k * ch:(k + 1) * ch].astype(F32)
+        first[k * ch:(k + 1) * ch, :] = sums[:, wide + k * ch:wide + (k + 1) * ch].astype(F32)
+    head[...] = sums[:, 2 * wide:].astype(F32).T[0:head.shape[0], :]
+    loss[0] = mean[0, 0]
+
+
+def spread(sums, mean, traits):
+    ch = sums.shape[0]
+    wide = (sums.shape[1] - 128) // 2
+    vmem = pl.BlockSpec(memory_space=pltpu.VMEM)
+    smem = pl.BlockSpec(memory_space=pltpu.SMEM)
+    return pl.pallas_call(
+        spread_kernel,
+        out_shape=[
+            jax.ShapeDtypeStruct((wide, ch), F32),
+            jax.ShapeDtypeStruct((wide, ch), F32),
+            jax.ShapeDtypeStruct((traits, ch), F32),
+            jax.ShapeDtypeStruct((1,), F32),
+        ],
+        in_specs=[vmem, smem],
+        out_specs=[vmem, vmem, vmem, smem],
+        compiler_params=pltpu.CompilerParams(vmem_limit_bytes=62 * 2**20),
+    )(sums, mean)
 
 
 def summed(g1, g2, gh, err, share):
@@ -353,13 +380,11 @@
     return pl.pallas_call(
         functools.partial(total_kernel, share),
         out_shape=[
-            jax.ShapeDtypeStruct((ch, wide), F32),
-            jax.ShapeDtypeStruct((ch, wide), F32),
-            jax.ShapeDtypeStruct((128, ch), F32),
+            jax.ShapeDtypeStruct((ch, every), BF),
             jax.ShapeDtypeStruct((8, 128), F32),
         ],
         in_specs=[pl.BlockSpec(memory_space=pltpu.HBM)] * 4,
-        out_specs=[vmem] * 4,
+        out_specs=[vmem] * 2,
         scratch_shapes=[
             pltpu.VMEM((ch, wide), F32), pltpu.VMEM((ch, wide), F32), pltpu.VMEM((ch, 128), F32),
             pltpu.VMEM(err.shape, F32), pltpu.SemaphoreType.DMA((4,)),
@@ -439,17 +464,15 @@
     hidden, gfeat, g1, g2, gh, err = local(
         features, flo, fhi, seg, tgt, tlo, thi, w_first, w_second, wht, 1.0 / every**0.5)
     if count == 16 and ch == 256:
-        g1, g2, ght, mean = summed(g1, g2, gh, err, 1.0 / (every * traits))
-        loss = mean[0, 0:1]
-    else:
-        g1, g2, gh, err = lax.psum((g1, g2, gh, err), "tm")
-        ght = gh.T
-        loss = jnp.reshape(jnp.sum(err) / (every * traits), (1,))
+        first, second, head, loss = spread(*summed(g1, g2, gh, err, 1.0 / (every * traits)), traits)
+        return hidden, gfeat, first, second, head.T, loss
 
     def taps(g):
         return jnp.concatenate([g[:, k * ch:(k + 1) * ch] for k in range(3)], 0)
 
-    return hidden, gfeat, taps(g1), taps(g2), ght[:traits].T, loss
+    g1, g2, gh, err = lax.psum((g1, g2, gh, err), "tm")
+    loss = jnp.reshape(jnp.sum(err) / (every * traits), (1,))
+    return hidden, gfeat, taps(g1), taps(g2), gh[:, :traits], loss
 
 
 def solution(mesh):

time: 66.2 us -> 62.3 us (0.941)
  local copies, waits for them, and re-layouts: 4.03 us -> 0 us
  Pallas kernels: 59.3 us -> 61.4 us
  other arithmetic: 1.86 us -> 0 us
    slice x2 -> x0, local copies, waits for them, and re-layouts: 2.65 us -> none  [the longest x1 1.46 us: taps(): return jnp.concatenate([g[:, k * ch:(k + 1) * ch] for k in range(3)], 0)]
    pallas_call x0 -> x1, Pallas kernels: none -> 2.37 us  [spread(): pl.pallas_call(spread_kernel, out_shape=[jax.ShapeDtypeStruct((wide, ch),...]
    concatenate x2 -> x0, other arithmetic: 1.86 us -> none  [taps(): return jnp.concatenate([g[:, k * ch:(k + 1) * ch] for k in range(3)], 0)]
    transpose x1 -> x0, local copies, waits for them, and re-layouts: 1.37 us -> none  [shards(): return (hidden, gfeat, taps(g1), taps(g2), ght[:traits].T, loss)]
where the time goes in v4:
time: 62.3 us; the launch traced here: 62.1 us
  Pallas kernels  61.4 us (99%)
  between operations  0.66 us (1%)
    pallas_call x1, Pallas kernels, summed(): pl.pallas_call(functools.partial(total_kernel, share), out_shape=[jax.Sha...  26.1 us
    pallas_call x1, Pallas kernels, local(): pl.pallas_call(functools.partial(compute, rows, scale), out_shape=[jax.Sh...  23.4 us
    pallas_call x1, Pallas kernels, halos(): pl.pallas_call(functools.partial(halo_kernel, lax.axis_size('tm')), out_s...  9.61 us
    pallas_call x1, Pallas kernels, spread(): pl.pallas_call(spread_kernel, out_shape=[jax.ShapeDtypeStruct((wide, ch),...  2.37 us

profile of v4, /device:TPU:0, one launch (start us, length us, event | category | flops | bytes accessed | tf_op | source)
XLA Modules:
  0.0 62.1 jit_solution(10694318184170969784)
XLA Ops:
  0.6 9.6 %shard_map.109 = (bf16[64,256]{1,0:T(8,128)(2,1)}, bf16[64,256]{1,0:T(8,128)(2,1)}, f32[32,128]{1,0:T(8,128)}, f32[32,128]{1,0:T(8,128)}, s32[34,128]{1,0:T(8,128)}) custom-call(bf16[4096,256]{1,0:T(8,128)(2,1)} %feat.3, s32[32,128]{1,0:T(8,128)} %bitcast.6, f32[32,4096]{1,0:T(8,128)} %bitcast.4), custom_call_target="tpu_custom_call" | custom-call | tf_op jit(solution)/shard_map/pallas_call | solution.py:446
  10.2 23.4 %shard_map.110 = (bf16[4096,256]{1,0:T(8,128)(2,1)}, bf16[4096,256]{1,0:T(8,128)(2,1)}, f32[256,768]{1,0:T(8,128)}, f32[256,768]{1,0:T(8,128)}, f32[256,128]{1,0:T(8,128)}, /*index=5*/f32[32,128]{1,0:T(8,128)}) custom-call(bf16[4096,256]{1,0:T(8,128)(2,1)} %feat.3, bf16[64,256]{1,0:T(8,128)(2,1)} %get-tuple-element.23.flo, ...), custom_call_target="tpu_custom_call" | custom-call | flops 10737418240 | bytes 8388608 | tf_op jit(solution)/shard_map/pallas_call | solution.py:183
  33.6 26.1 %shard_map.111 = (bf16[256,1664]{1,0:T(8,128)(2,1)}, f32[8,128]{1,0:T(8,128)}) custom-call(f32[256,768]{1,0:T(8,128)} %get-tuple-element.30.h1, f32[256,768]{1,0:T(8,128)} %get-tuple-element.31.h2, f32[256,128]{1,0:T(8,128)} %get-tuple-element.32.hh, f32[32,128]{1,0:T(8,128)} %get-tuple-element.33.he), custom_call_target="tpu_custom_call" | custom-call | tf_op jit(solution)/shard_map/pallas_call | solution.py:380
  59.7 2.4 %shard_map.112 = (f32[768,256]{1,0:T(8,128)}, f32[768,256]{1,0:T(8,128)}, f32[32,256]{1,0:T(8,128)}, f32[1]{0:T(128)}) custom-call(bf16[256,1664]{1,0:T(8,128)(2,1)} %get-tuple-element.34.sums, f32[8,128]{1,0:T(8,128)} %get-tuple-element.35.mean), custom_call_target="tpu_custom_call" | custom-call | tf_op jit(solution)/shard_map/pallas_call | solution.py:362
